TPU v7x, 1024 devices: a whole 4x4x32 slice. The times are simulated.
1024 devices in a mesh: row: 32 (over z_hi, y, core), col: 32 (over z_lo, x).
Axes of the slice: x: 4, y: 4, z: 32 (z_hi: 4, z_lo: 8; z = z_hi * 8 + z_lo), core: 2. Of those that a mesh axis runs over, the one named last changes fastest.
Arguments:
- a_blocks: bfloat16 [128, 4096, 128], P('row', 'col'), may hold values from -0.5 to 0.5
- a_coord: int32 [32, 128], P('row', 'col'), may hold values from 0 to 15, as said below
- a_count: int32 [32, 32], P('row', 'col'), may hold values from 1 to 4, as said below
- b_blocks: bfloat16 [128, 4096, 128], P('row', 'col'), may hold values from -6 to 6
- b_coord: int32 [32, 128], P('row', 'col'), may hold values from 0 to 15, as said below
- b_count: int32 [32, 32], P('row', 'col'), may hold values from 1 to 4, as said below
- c_pattern: int32 [128, 128], P('row', 'col'), may hold values 0 or 1
Outputs:
- product: bfloat16 [16384, 16384], P('row', 'col')
Inputs may be any that keep to these rules, and one draw needn't show every extreme that they name: `a_coord`: in each panel the codes of all 4 slots are distinct. `b_coord`: in each panel the codes of all 4 slots are distinct. `a_count`: some panel is full. `b_count`: some panel is full.
All inputs are finite; a program needn't handle non-finite values. No bound on the sum of `c_pattern` on one device may be relied on, other than what follows from the above.
Results may differ from a plain program's by a relative error of at most 0.001.
Values may be sent and summed in bfloat16 or wider, within the bound.
A program may use at most 32 MiB of HBM per device.

v0:
```python
import jax
import jax.numpy as jnp
from jax import lax
from jax.sharding import PartitionSpec as P

STEPS = 4


def for_sending(array):

    def short(part):
        return part.astype(jnp.bfloat16) if part.dtype == jnp.float32 else part

    return jax.tree.map(short, array)


def from_behind(value, axis, steps):
    count = lax.axis_size(axis)
    pairs = [(source, (source + steps) % count) for source in range(count)]
    return lax.ppermute(value, axis, pairs)


def panel_product(a_blocks, a_code, a_live_count, b_blocks, b_code, b_live_count, pattern):
    width = pattern.shape[0]
    slots_a = jnp.arange(a_blocks.shape[0], dtype=jnp.int32)
    slots_b = jnp.arange(b_blocks.shape[0], dtype=jnp.int32)
    places = jnp.arange(width, dtype=jnp.int32)
    a_live = (slots_a < a_live_count).astype(jnp.float32)
    b_live = (slots_b < b_live_count).astype(jnp.float32)
    a_row = a_code // width
    a_col = a_code % width
    b_row = b_code // width
    b_col = b_code % width
    row_hot = (a_row[:, None] == places[None, :]).astype(jnp.float32) * a_live[:, None]
    col_hot = (b_col[:, None] == places[None, :]).astype(jnp.float32) * b_live[:, None]
    linked = (a_col[:, None] == b_row[None, :]).astype(jnp.float32)
    kept = jnp.dot(
        jnp.dot(row_hot, pattern.astype(jnp.float32), precision=lax.Precision.HIGHEST),
        col_hot.T,
        precision=lax.Precision.HIGHEST,
    )
    weight = linked * kept
    products = jnp.einsum("aik,bkj->abij", a_blocks, b_blocks, preferred_element_type=jnp.float32)
    scaled = products * weight[:, :, None, None]
    partial_rows = jnp.einsum("ar,abij->rbij", row_hot, scaled, precision=lax.Precision.HIGHEST)
    return jnp.einsum("bc,rbij->ricj", col_hot, partial_rows, precision=lax.Precision.HIGHEST)


def choose(take, moved, kept):
    return jax.tree.map(
        lambda new_value, old_value: jnp.where(take, new_value, old_value), moved, kept
    )


def per_device(a_blocks, a_coord, a_count, b_blocks, b_coord, b_count, c_pattern):
    width = c_pattern.shape[0]
    block = a_blocks.shape[1]
    rows_total = lax.axis_size("row")
    row_at = lax.axis_index("row")
    col_low = lax.axis_index("col") % rows_total
    total = jnp.zeros((width, block, width, block), jnp.float32)
    a_state = (a_blocks, a_coord, a_count)
    b_state = (b_blocks, b_coord, b_count)
    depth = (rows_total - 1).bit_length()
    for bit in range(depth):
        moved_a = from_behind(
            (a_state[0], for_sending(a_state[1]), for_sending(a_state[2])), "col", -(1 << bit)
        )
        a_state = choose(jnp.right_shift(row_at, bit) % 2 == 1, moved_a, a_state)
        moved_b = from_behind(
            (b_state[0], for_sending(b_state[1]), for_sending(b_state[2])), "row", -(1 << bit)
        )
        b_state = choose(jnp.right_shift(col_low, bit) % 2 == 1, moved_b, b_state)
    for step in range(STEPS):
        total = total + panel_product(
            a_state[0],
            a_state[1][0],
            a_state[2][0, 0],
            b_state[0],
            b_state[1][0],
            b_state[2][0, 0],
            c_pattern,
        )
        if step + 1 < STEPS:
            a_state = from_behind(
                (a_state[0], for_sending(a_state[1]), for_sending(a_state[2])), "col", -1
            )
            b_state = from_behind(
                (b_state[0], for_sending(b_state[1]), for_sending(b_state[2])), "row", -1
            )
    return total.reshape(width * block, width * block).astype(jnp.bfloat16)


def solution(mesh):
    placed = (
        P("row", "col", None),
        P("row", "col"),
        P("row", "col"),
        P("row", "col", None),
        P("row", "col"),
        P("row", "col"),
        P("row", "col"),
    )
    return jax.shard_map(
        per_device, mesh=mesh, in_specs=placed, out_specs=P("row", "col"), check_vma=False
    )
```

profile of v0, /device:TPU:68, one launch (start us, length us, event | category | flops | bytes accessed | tf_op | source)
XLA Modules:
  0.0 511.4 jit_solution(15337513852881327443)
XLA Ops:
  0.0 23.1 %collective-permute-start.10 = (bf16[4,128,128]{2,1,0:T(8,128)(2,1)}, bf16[4,128,128]{2,1,0:T(8,128)(2,1)S(1)}, u32[]{:S(2)}, u32[]{:S(2)}) collective-permute-start(bf16[4,128,128]{2,1,0:T(8,128)(2,1)} %param.10), channel_id=1, source_target_pairs={{0,992},{32,0},{64,32},{96,64},{128,96},{160,128},{192,160},{224,1... | collective-permute-start | bytes 393224 | tf_op jit(solution)/shard_map/ppermute | solution.py:20
  28.0 5.1 collective-permute-start
  59.5 10.8 %collective-permute-start.27 = (s32[1,1]{1,0:T(1,128)}, s32[1,1]{1,0:T(1,128)}, u32[]{:S(2)}, u32[]{:S(2)}) collective-permute-start(s32[1,1]{1,0:T(1,128)} %select_n.416), channel_id=1, source_target_pairs={{0,896},{32,928},{64,960},{96,992},{128,0},{160,32},{192,64},{224,... | collective-permute-start | bytes 20 | tf_op jit(solution)/shard_map/ppermute | solution.py:20
  71.0 13.0 %collective-permute-start.8 = (s32[1,1]{1,0:T(1,128)}, s32[1,1]{1,0:T(1,128)}, u32[]{:S(2)}, u32[]{:S(2)}) collective-permute-start(s32[1,1]{1,0:T(1,128)} %select_n.368), channel_id=1, source_target_pairs={{0,24},{1,25},{2,26},{3,27},{4,28},{5,29},{6,30},{7,31},{8,0},{9,1... | collective-permute-start | bytes 20 | tf_op jit(solution)/shard_map/ppermute | solution.py:20
  84.5 6.7 %collective-permute-start.28 = (s32[1,1]{1,0:T(1,128)}, s32[1,1]{1,0:T(1,128)}, u32[]{:S(2)}, u32[]{:S(2)}) collective-permute-start(s32[1,1]{1,0:T(1,128)} %select_n.417), channel_id=1, source_target_pairs={{0,768},{32,800},{64,832},{96,864},{128,896},{160,928},{192,960},{... | collective-permute-start | bytes 20 | tf_op jit(solution)/shard_map/ppermute | solution.py:20
  91.9 8.6 %collective-permute-start.9 = (s32[1,1]{1,0:T(1,128)}, s32[1,1]{1,0:T(1,128)}, u32[]{:S(2)}, u32[]{:S(2)}) collective-permute-start(s32[1,1]{1,0:T(1,128)} %select_n.369), channel_id=1, source_target_pairs={{0,16},{1,17},{2,18},{3,19},{4,20},{5,21},{6,22},{7,23},{8,24},{9,... | collective-permute-start | bytes 20 | tf_op jit(solution)/shard_map/ppermute | solution.py:20
  103.1 14.0 %collective-permute-start.29 = (s32[1,1]{1,0:T(1,128)}, s32[1,1]{1,0:T(1,128)}, u32[]{:S(2)}, u32[]{:S(2)}) collective-permute-start(s32[1,1]{1,0:T(1,128)} %select_n.418), channel_id=1, source_target_pairs={{0,512},{32,544},{64,576},{96,608},{128,640},{160,672},{192,704},{... | collective-permute-start | bytes 20 | tf_op jit(solution)/shard_map/ppermute | solution.py:20
  117.1 15.4 %collective-permute-start.21 = (s32[1,4]{1,0:T(1,128)S(1)}, s32[1,4]{1,0:T(1,128)S(1)}, u32[]{:S(2)}, u32[]{:S(2)}) collective-permute-start(s32[1,4]{1,0:T(1,128)S(1)} %broadcast_select_fusion.10), channel_id=1, source_target_pairs={{0,960},{32,992},{64,0},{96,32},{128,64},{160,96},{192,128},{224,1... | collective-permute-start | bytes 56 | tf_op jit(solution)/shard_map/ppermute | solution.py:20
  133.1 16.1 %collective-permute-start.31 = (s32[1,1]{1,0:T(1,128)}, s32[1,1]{1,0:T(1,128)}, u32[]{:S(2)}, u32[]{:S(2)}) collective-permute-start(s32[1,1]{1,0:T(1,128)} %select_n.370), channel_id=1, source_target_pairs={{0,31},{1,0},{2,1},{3,2},{4,3},{5,4},{6,5},{7,6},{8,7},{9,8},{10,9... | collective-permute-start | bytes 20 | tf_op jit(solution)/shard_map/ppermute | solution.py:20
  149.8 4.8 collective-permute-start.35
  155.9 5.3 %collective-permute-start.37 = (s32[1,1]{1,0:T(1,128)}, s32[1,1]{1,0:T(1,128)}, u32[]{:S(2)}, u32[]{:S(2)}) collective-permute-start(s32[1,1]{1,0:T(1,128)} %collective-permute-done.31), channel_id=1, source_target_pairs={{0,31},{1,0},{2,1},{3,2},{4,3},{5,4},{6,5},{7,6},{8,7},{9,8},{10,9... | collective-permute-start | bytes 20 | tf_op jit(solution)/shard_map/ppermute | solution.py:20
  162.6 13.2 %collective-permute-start.41 = (s32[1,1]{1,0:T(1,128)}, s32[1,1]{1,0:T(1,128)}, u32[]{:S(2)}, u32[]{:S(2)}) collective-permute-start(s32[1,1]{1,0:T(1,128)} %collective-permute-done.35), channel_id=1, source_target_pairs={{0,992},{32,0},{64,32},{96,64},{128,96},{160,128},{192,160},{224,1... | collective-permute-start | bytes 20 | tf_op jit(solution)/shard_map/ppermute | solution.py:20
  181.7 14.1 %collective-permute-start.47 = (s32[1,1]{1,0:T(1,128)}, s32[1,1]{1,0:T(1,128)}, u32[]{:S(2)}, u32[]{:S(2)}) collective-permute-start(s32[1,1]{1,0:T(1,128)} %collective-permute-done.41), channel_id=1, source_target_pairs={{0,992},{32,0},{64,32},{96,64},{128,96},{160,128},{192,160},{224,1... | collective-permute-start | bytes 20 | tf_op jit(solution)/shard_map/ppermute | solution.py:20
  205.9 11.8 %collective-permute-start.3 = (s32[1,4]{1,0:T(1,128)S(1)}, s32[1,4]{1,0:T(1,128)S(1)}, u32[]{:S(2)}, u32[]{:S(2)}) collective-permute-start(s32[1,4]{1,0:T(1,128)S(1)} %broadcast_select_fusion.17), channel_id=1, source_target_pairs={{0,24},{1,25},{2,26},{3,27},{4,28},{5,29},{6,30},{7,31},{8,0},{9,1... | collective-permute-start | bytes 56 | tf_op jit(solution)/shard_map/ppermute | solution.py:20
  217.8 8.5 %collective-permute-start.23 = (s32[1,4]{1,0:T(1,128)S(1)}, s32[1,4]{1,0:T(1,128)S(1)}, u32[]{:S(2)}, u32[]{:S(2)}) collective-permute-start(s32[1,4]{1,0:T(1,128)S(1)} %broadcast_select_fusion.12), channel_id=1, source_target_pairs={{0,768},{32,800},{64,832},{96,864},{128,896},{160,928},{192,960},{... | collective-permute-start | bytes 56 | tf_op jit(solution)/shard_map/ppermute | solution.py:20
  231.9 11.4 %collective-permute-start.24 = (s32[1,4]{1,0:T(1,128)S(1)}, s32[1,4]{1,0:T(1,128)S(1)}, u32[]{:S(2)}, u32[]{:S(2)}) collective-permute-start(s32[1,4]{1,0:T(1,128)S(1)} %broadcast_select_fusion.13), channel_id=1, source_target_pairs={{0,512},{32,544},{64,576},{96,608},{128,640},{160,672},{192,704},{... | collective-permute-start | bytes 56 | tf_op jit(solution)/shard_map/ppermute | solution.py:20
  247.0 8.6 %collective-permute-done.24 = s32[1,4]{1,0:T(1,128)S(1)} collective-permute-done((s32[1,4]{1,0:T(1,128)S(1)}, s32[1,4]{1,0:T(1,128)S(1)}, u32[]{:S(2)}, u32[]{:S(2)}) %collective-permute-start.24) | collective-permute-done | bytes 48 | tf_op jit(solution)/shard_map/ppermute | solution.py:20
  259.7 11.2 %collective-permute-start.36 = (s32[1,4]{1,0:T(1,128)S(1)}, s32[1,4]{1,0:T(1,128)S(1)}, u32[]{:S(2)}, u32[]{:S(2)}) collective-permute-start(s32[1,4]{1,0:T(1,128)S(1)} %collective-permute-done.30), channel_id=1, source_target_pairs={{0,31},{1,0},{2,1},{3,2},{4,3},{5,4},{6,5},{7,6},{8,7},{9,8},{10,9... | collective-permute-start | bytes 56 | tf_op jit(solution)/shard_map/ppermute | solution.py:20
  270.8 14.1 %collective-permute-start.40 = (s32[1,4]{1,0:T(1,128)S(1)}, s32[1,4]{1,0:T(1,128)S(1)}, u32[]{:S(2)}, u32[]{:S(2)}) collective-permute-start(s32[1,4]{1,0:T(1,128)S(1)} %collective-permute-done.34), channel_id=1, source_target_pairs={{0,992},{32,0},{64,32},{96,64},{128,96},{160,128},{192,160},{224,1... | collective-permute-start | bytes 56 | tf_op jit(solution)/shard_map/ppermute | solution.py:20
  286.9 11.7 %collective-permute-start.42 = (s32[1,4]{1,0:T(1,128)S(1)}, s32[1,4]{1,0:T(1,128)S(1)}, u32[]{:S(2)}, u32[]{:S(2)}) collective-permute-start(s32[1,4]{1,0:T(1,128)S(1)} %collective-permute-done.36), channel_id=1, source_target_pairs={{0,31},{1,0},{2,1},{3,2},{4,3},{5,4},{6,5},{7,6},{8,7},{9,8},{10,9... | collective-permute-start | bytes 56 | tf_op jit(solution)/shard_map/ppermute | solution.py:20
  298.6 14.1 %collective-permute-start.46 = (s32[1,4]{1,0:T(1,128)S(1)}, s32[1,4]{1,0:T(1,128)S(1)}, u32[]{:S(2)}, u32[]{:S(2)}) collective-permute-start(s32[1,4]{1,0:T(1,128)S(1)} %collective-permute-done.40), channel_id=1, source_target_pairs={{0,992},{32,0},{64,32},{96,64},{128,96},{160,128},{192,160},{224,1... | collective-permute-start | bytes 56 | tf_op jit(solution)/shard_map/ppermute | solution.py:20
  323.8 12.9 %collective-permute-done.16 = bf16[4,128,128]{2,1,0:T(8,128)(2,1)S(1)} collective-permute-done((bf16[4,128,128]{2,1,0:T(8,128)(2,1)S(1)}, bf16[4,128,128]{2,1,0:T(8,128)(2,1)S(1)}, u32[]{:S(2)}, u32[]{:S(2)}) %collective-permute-start.16) | collective-permute-done | bytes 131104 | tf_op jit(solution)/shard_map/ppermute | solution.py:20
  338.7 11.9 %collective-permute-start.13 = (bf16[4,128,128]{2,1,0:T(8,128)(2,1)S(1)}, bf16[4,128,128]{2,1,0:T(8,128)(2,1)S(1)}, u32[]{:S(2)}, u32[]{:S(2)}) collective-permute-start(bf16[4,128,128]{2,1,0:T(8,128)(2,1)S(1)} %broadcast_select_fusion.7), channel_id=1, source_target_pairs={{0,768},{32,800},{64,832},{96,864},{128,896},{160,928},{192,960},{... | collective-permute-start | bytes 393224 | tf_op jit(solution)/shard_map/ppermute | solution.py:20
  350.6 5.7 %collective-permute-done.17 = bf16[4,128,128]{2,1,0:T(8,128)(2,1)S(1)} collective-permute-done((bf16[4,128,128]{2,1,0:T(8,128)(2,1)S(1)}, bf16[4,128,128]{2,1,0:T(8,128)(2,1)S(1)}, u32[]{:S(2)}, u32[]{:S(2)}) %collective-permute-start.17) | collective-permute-done | bytes 131104 | tf_op jit(solution)/shard_map/ppermute | solution.py:20
  356.4 8.2 %collective-permute-start.18 = (bf16[4,128,128]{2,1,0:T(8,128)(2,1)S(1)}, bf16[4,128,128]{2,1,0:T(8,128)(2,1)S(1)}, u32[]{:S(2)}, u32[]{:S(2)}) collective-permute-start(bf16[4,128,128]{2,1,0:T(8,128)(2,1)S(1)} %broadcast_select_fusion.2), channel_id=1, source_target_pairs={{0,24},{1,25},{2,26},{3,27},{4,28},{5,29},{6,30},{7,31},{8,0},{9,1... | collective-permute-start | bytes 393224 | tf_op jit(solution)/shard_map/ppermute | solution.py:20
  364.5 8.6 %collective-permute-done.13 = bf16[4,128,128]{2,1,0:T(8,128)(2,1)S(1)} collective-permute-done((bf16[4,128,128]{2,1,0:T(8,128)(2,1)S(1)}, bf16[4,128,128]{2,1,0:T(8,128)(2,1)S(1)}, u32[]{:S(2)}, u32[]{:S(2)}) %collective-permute-start.13) | collective-permute-done | bytes 131104 | tf_op jit(solution)/shard_map/ppermute | solution.py:20
  373.1 16.7 %collective-permute-start.14 = (bf16[4,128,128]{2,1,0:T(8,128)(2,1)S(1)}, bf16[4,128,128]{2,1,0:T(8,128)(2,1)S(1)}, u32[]{:S(2)}, u32[]{:S(2)}) collective-permute-start(bf16[4,128,128]{2,1,0:T(8,128)(2,1)S(1)} %broadcast_select_fusion.8), channel_id=1, source_target_pairs={{0,512},{32,544},{64,576},{96,608},{128,640},{160,672},{192,704},{... | collective-permute-start | bytes 393224 | tf_op jit(solution)/shard_map/ppermute | solution.py:20
  390.1 7.8 %collective-permute-start.19 = (bf16[4,128,128]{2,1,0:T(8,128)(2,1)S(1)}, bf16[4,128,128]{2,1,0:T(8,128)(2,1)S(1)}, u32[]{:S(2)}, u32[]{:S(2)}) collective-permute-start(bf16[4,128,128]{2,1,0:T(8,128)(2,1)S(1)} %broadcast_select_fusion.3), channel_id=1, source_target_pairs={{0,16},{1,17},{2,18},{3,19},{4,20},{5,21},{6,22},{7,23},{8,24},{9,... | collective-permute-start | bytes 393224 | tf_op jit(solution)/shard_map/ppermute | solution.py:20
  397.9 6.2 %collective-permute-done.14 = bf16[4,128,128]{2,1,0:T(8,128)(2,1)S(1)} collective-permute-done((bf16[4,128,128]{2,1,0:T(8,128)(2,1)S(1)}, bf16[4,128,128]{2,1,0:T(8,128)(2,1)S(1)}, u32[]{:S(2)}, u32[]{:S(2)}) %collective-permute-start.14) | collective-permute-done | bytes 131104 | tf_op jit(solution)/shard_map/ppermute | solution.py:20
  404.1 42.8 %collective-permute-start.32 = (bf16[4,128,128]{2,1,0:T(8,128)(2,1)S(1)}, bf16[4,128,128]{2,1,0:T(8,128)(2,1)S(1)}, u32[]{:S(2)}, u32[]{:S(2)}) collective-permute-start(bf16[4,128,128]{2,1,0:T(8,128)(2,1)S(1)} %broadcast_select_fusion.9), channel_id=1, source_target_pairs={{0,992},{32,0},{64,32},{96,64},{128,96},{160,128},{192,160},{224,1... | collective-permute-start | bytes 393224 | tf_op jit(solution)/shard_map/ppermute | solution.py:20
  459.3 12.0 %collective-permute-start.38 = (bf16[4,128,128]{2,1,0:T(8,128)(2,1)S(1)}, bf16[4,128,128]{2,1,0:T(8,128)(2,1)S(1)}, u32[]{:S(2)}, u32[]{:S(2)}) collective-permute-start(bf16[4,128,128]{2,1,0:T(8,128)(2,1)S(1)} %collective-permute-done.32), channel_id=1, source_target_pairs={{0,992},{32,0},{64,32},{96,64},{128,96},{160,128},{192,160},{224,1... | collective-permute-start | bytes 393224 | tf_op jit(solution)/shard_map/ppermute | solution.py:20
  482.6 14.9 %collective-permute-start.44 = (bf16[4,128,128]{2,1,0:T(8,128)(2,1)S(1)}, bf16[4,128,128]{2,1,0:T(8,128)(2,1)S(1)}, u32[]{:S(2)}, u32[]{:S(2)}) collective-permute-start(bf16[4,128,128]{2,1,0:T(8,128)(2,1)S(1)} %collective-permute-done.38), channel_id=1, source_target_pairs={{0,992},{32,0},{64,32},{96,64},{128,96},{160,128},{192,160},{224,1... | collective-permute-start | bytes 393224 | tf_op jit(solution)/shard_map/ppermute | solution.py:20
  (194 shorter events, 113.6 us)
Async XLA Ops:
  0.0 314.8 %collective-permute-start.10 = (bf16[4,128,128]{2,1,0:T(8,128)(2,1)}, bf16[4,128,128]{2,1,0:T(8,128)(2,1)S(1)}, u32[]{:S(2)}, u32[]{:S(2)}) collective-permute-start(bf16[4,128,128]{2,1,0:T(8,128)(2,1)} %param.10), channel_id=1, source_target_pairs={{0,992},{32,0},{64,32},{96,64},{128,96},{160,128},{192,160},{224,1... | collective-permute-start | bytes 393224 | tf_op jit(solution)/shard_map/ppermute | solution.py:20
  23.1 293.9 %collective-permute-start.15 = (bf16[4,128,128]{2,1,0:T(8,128)(2,1)}, bf16[4,128,128]{2,1,0:T(8,128)(2,1)S(1)}, u32[]{:S(2)}, u32[]{:S(2)}) collective-permute-start(bf16[4,128,128]{2,1,0:T(8,128)(2,1)} %param.7), channel_id=1, source_target_pairs={{0,31},{1,0},{2,1},{3,2},{4,3},{5,4},{6,5},{7,6},{8,7},{9,8},{10,9... | collective-permute-start | bytes 393224 | tf_op jit(solution)/shard_map/ppermute | solution.py:20
  28.0 63.9 %collective-permute-start = (s32[1,4]{1,0:T(1,128)}, s32[1,4]{1,0:T(1,128)S(1)}, u32[]{:S(2)}, u32[]{:S(2)}) collective-permute-start(s32[1,4]{1,0:T(1,128)} %param.8), channel_id=1, source_target_pairs={{0,31},{1,0},{2,1},{3,2},{4,3},{5,4},{6,5},{7,6},{8,7},{9,8},{10,9... | collective-permute-start | bytes 56 | tf_op jit(solution)/shard_map/ppermute | solution.py:20
  37.1 65.9 %collective-permute-start.20 = (s32[1,4]{1,0:T(1,128)S(1)}, s32[1,4]{1,0:T(1,128)S(1)}, u32[]{:S(2)}, u32[]{:S(2)}) collective-permute-start(s32[1,4]{1,0:T(1,128)S(1)} %copy-done.13), channel_id=1, source_target_pairs={{0,992},{32,0},{64,32},{96,64},{128,96},{160,128},{192,160},{224,1... | collective-permute-start | bytes 56 | tf_op jit(solution)/shard_map/ppermute | solution.py:20
  84.5 16.0 %collective-permute-start.28 = (s32[1,1]{1,0:T(1,128)}, s32[1,1]{1,0:T(1,128)}, u32[]{:S(2)}, u32[]{:S(2)}) collective-permute-start(s32[1,1]{1,0:T(1,128)} %select_n.417), channel_id=1, source_target_pairs={{0,768},{32,800},{64,832},{96,864},{128,896},{160,928},{192,960},{... | collective-permute-start | bytes 20 | tf_op jit(solution)/shard_map/ppermute | solution.py:20
  91.9 25.2 %collective-permute-start.9 = (s32[1,1]{1,0:T(1,128)}, s32[1,1]{1,0:T(1,128)}, u32[]{:S(2)}, u32[]{:S(2)}) collective-permute-start(s32[1,1]{1,0:T(1,128)} %select_n.369), channel_id=1, source_target_pairs={{0,16},{1,17},{2,18},{3,19},{4,20},{5,21},{6,22},{7,23},{8,24},{9,... | collective-permute-start | bytes 20 | tf_op jit(solution)/shard_map/ppermute | solution.py:20
  100.6 81.1 %collective-permute-start.1 = (s32[1,4]{1,0:T(1,128)S(1)}, s32[1,4]{1,0:T(1,128)S(1)}, u32[]{:S(2)}, u32[]{:S(2)}) collective-permute-start(s32[1,4]{1,0:T(1,128)S(1)} %broadcast_select_fusion.15), channel_id=1, source_target_pairs={{0,30},{1,31},{2,0},{3,1},{4,2},{5,3},{6,4},{7,5},{8,6},{9,7},{10,... | collective-permute-start | bytes 56 | tf_op jit(solution)/shard_map/ppermute | solution.py:20
  103.1 30.1 %collective-permute-start.29 = (s32[1,1]{1,0:T(1,128)}, s32[1,1]{1,0:T(1,128)}, u32[]{:S(2)}, u32[]{:S(2)}) collective-permute-start(s32[1,1]{1,0:T(1,128)} %select_n.418), channel_id=1, source_target_pairs={{0,512},{32,544},{64,576},{96,608},{128,640},{160,672},{192,704},{... | collective-permute-start | bytes 20 | tf_op jit(solution)/shard_map/ppermute | solution.py:20
  117.1 78.7 %collective-permute-start.21 = (s32[1,4]{1,0:T(1,128)S(1)}, s32[1,4]{1,0:T(1,128)S(1)}, u32[]{:S(2)}, u32[]{:S(2)}) collective-permute-start(s32[1,4]{1,0:T(1,128)S(1)} %broadcast_select_fusion.10), channel_id=1, source_target_pairs={{0,960},{32,992},{64,0},{96,32},{128,64},{160,96},{192,128},{224,1... | collective-permute-start | bytes 56 | tf_op jit(solution)/shard_map/ppermute | solution.py:20
  133.1 16.7 %collective-permute-start.31 = (s32[1,1]{1,0:T(1,128)}, s32[1,1]{1,0:T(1,128)}, u32[]{:S(2)}, u32[]{:S(2)}) collective-permute-start(s32[1,1]{1,0:T(1,128)} %select_n.370), channel_id=1, source_target_pairs={{0,31},{1,0},{2,1},{3,2},{4,3},{5,4},{6,5},{7,6},{8,7},{9,8},{10,9... | collective-permute-start | bytes 20 | tf_op jit(solution)/shard_map/ppermute | solution.py:20
  162.6 14.5 %collective-permute-start.41 = (s32[1,1]{1,0:T(1,128)}, s32[1,1]{1,0:T(1,128)}, u32[]{:S(2)}, u32[]{:S(2)}) collective-permute-start(s32[1,1]{1,0:T(1,128)} %collective-permute-done.35), channel_id=1, source_target_pairs={{0,992},{32,0},{64,32},{96,64},{128,96},{160,128},{192,160},{224,1... | collective-permute-start | bytes 20 | tf_op jit(solution)/shard_map/ppermute | solution.py:20
  177.7 20.4 %collective-permute-start.43 = (s32[1,1]{1,0:T(1,128)}, s32[1,1]{1,0:T(1,128)}, u32[]{:S(2)}, u32[]{:S(2)}) collective-permute-start(s32[1,1]{1,0:T(1,128)} %collective-permute-done.37), channel_id=1, source_target_pairs={{0,31},{1,0},{2,1},{3,2},{4,3},{5,4},{6,5},{7,6},{8,7},{9,8},{10,9... | collective-permute-start | bytes 20 | tf_op jit(solution)/shard_map/ppermute | solution.py:20
  181.7 19.0 %collective-permute-start.47 = (s32[1,1]{1,0:T(1,128)}, s32[1,1]{1,0:T(1,128)}, u32[]{:S(2)}, u32[]{:S(2)}) collective-permute-start(s32[1,1]{1,0:T(1,128)} %collective-permute-done.41), channel_id=1, source_target_pairs={{0,992},{32,0},{64,32},{96,64},{128,96},{160,128},{192,160},{224,1... | collective-permute-start | bytes 20 | tf_op jit(solution)/shard_map/ppermute | solution.py:20
  198.1 19.6 %collective-permute-start.22 = (s32[1,4]{1,0:T(1,128)S(1)}, s32[1,4]{1,0:T(1,128)S(1)}, u32[]{:S(2)}, u32[]{:S(2)}) collective-permute-start(s32[1,4]{1,0:T(1,128)S(1)} %broadcast_select_fusion.11), channel_id=1, source_target_pairs={{0,896},{32,928},{64,960},{96,992},{128,0},{160,32},{192,64},{224,... | collective-permute-start | bytes 56 | tf_op jit(solution)/shard_map/ppermute | solution.py:20
  205.9 20.3 %collective-permute-start.3 = (s32[1,4]{1,0:T(1,128)S(1)}, s32[1,4]{1,0:T(1,128)S(1)}, u32[]{:S(2)}, u32[]{:S(2)}) collective-permute-start(s32[1,4]{1,0:T(1,128)S(1)} %broadcast_select_fusion.17), channel_id=1, source_target_pairs={{0,24},{1,25},{2,26},{3,27},{4,28},{5,29},{6,30},{7,31},{8,0},{9,1... | collective-permute-start | bytes 56 | tf_op jit(solution)/shard_map/ppermute | solution.py:20
  226.2 17.1 %collective-permute-start.4 = (s32[1,4]{1,0:T(1,128)S(1)}, s32[1,4]{1,0:T(1,128)S(1)}, u32[]{:S(2)}, u32[]{:S(2)}) collective-permute-start(s32[1,4]{1,0:T(1,128)S(1)} %broadcast_select_fusion.18), channel_id=1, source_target_pairs={{0,16},{1,17},{2,18},{3,19},{4,20},{5,21},{6,22},{7,23},{8,24},{9,... | collective-permute-start | bytes 56 | tf_op jit(solution)/shard_map/ppermute | solution.py:20
  231.9 23.7 %collective-permute-start.24 = (s32[1,4]{1,0:T(1,128)S(1)}, s32[1,4]{1,0:T(1,128)S(1)}, u32[]{:S(2)}, u32[]{:S(2)}) collective-permute-start(s32[1,4]{1,0:T(1,128)S(1)} %broadcast_select_fusion.13), channel_id=1, source_target_pairs={{0,512},{32,544},{64,576},{96,608},{128,640},{160,672},{192,704},{... | collective-permute-start | bytes 56 | tf_op jit(solution)/shard_map/ppermute | solution.py:20
  243.4 14.7 %collective-permute-start.30 = (s32[1,4]{1,0:T(1,128)S(1)}, s32[1,4]{1,0:T(1,128)S(1)}, u32[]{:S(2)}, u32[]{:S(2)}) collective-permute-start(s32[1,4]{1,0:T(1,128)S(1)} %get-tuple-element.8), channel_id=1, source_target_pairs={{0,31},{1,0},{2,1},{3,2},{4,3},{5,4},{6,5},{7,6},{8,7},{9,8},{10,9... | collective-permute-start | bytes 56 | tf_op jit(solution)/shard_map/ppermute | solution.py:20
  259.7 25.3 %collective-permute-start.36 = (s32[1,4]{1,0:T(1,128)S(1)}, s32[1,4]{1,0:T(1,128)S(1)}, u32[]{:S(2)}, u32[]{:S(2)}) collective-permute-start(s32[1,4]{1,0:T(1,128)S(1)} %collective-permute-done.30), channel_id=1, source_target_pairs={{0,31},{1,0},{2,1},{3,2},{4,3},{5,4},{6,5},{7,6},{8,7},{9,8},{10,9... | collective-permute-start | bytes 56 | tf_op jit(solution)/shard_map/ppermute | solution.py:20
  270.8 15.4 %collective-permute-start.40 = (s32[1,4]{1,0:T(1,128)S(1)}, s32[1,4]{1,0:T(1,128)S(1)}, u32[]{:S(2)}, u32[]{:S(2)}) collective-permute-start(s32[1,4]{1,0:T(1,128)S(1)} %collective-permute-done.34), channel_id=1, source_target_pairs={{0,992},{32,0},{64,32},{96,64},{128,96},{160,128},{192,160},{224,1... | collective-permute-start | bytes 56 | tf_op jit(solution)/shard_map/ppermute | solution.py:20
  286.9 25.8 %collective-permute-start.42 = (s32[1,4]{1,0:T(1,128)S(1)}, s32[1,4]{1,0:T(1,128)S(1)}, u32[]{:S(2)}, u32[]{:S(2)}) collective-permute-start(s32[1,4]{1,0:T(1,128)S(1)} %collective-permute-done.36), channel_id=1, source_target_pairs={{0,31},{1,0},{2,1},{3,2},{4,3},{5,4},{6,5},{7,6},{8,7},{9,8},{10,9... | collective-permute-start | bytes 56 | tf_op jit(solution)/shard_map/ppermute | solution.py:20
  298.6 15.4 %collective-permute-start.46 = (s32[1,4]{1,0:T(1,128)S(1)}, s32[1,4]{1,0:T(1,128)S(1)}, u32[]{:S(2)}, u32[]{:S(2)}) collective-permute-start(s32[1,4]{1,0:T(1,128)S(1)} %collective-permute-done.40), channel_id=1, source_target_pairs={{0,992},{32,0},{64,32},{96,64},{128,96},{160,128},{192,160},{224,1... | collective-permute-start | bytes 56 | tf_op jit(solution)/shard_map/ppermute | solution.py:20
  317.0 19.7 %collective-permute-start.16 = (bf16[4,128,128]{2,1,0:T(8,128)(2,1)S(1)}, bf16[4,128,128]{2,1,0:T(8,128)(2,1)S(1)}, u32[]{:S(2)}, u32[]{:S(2)}) collective-permute-start(bf16[4,128,128]{2,1,0:T(8,128)(2,1)S(1)} %broadcast_select_fusion), channel_id=1, source_target_pairs={{0,30},{1,31},{2,0},{3,1},{4,2},{5,3},{6,4},{7,5},{8,6},{9,7},{10,... | collective-permute-start | bytes 393224 | tf_op jit(solution)/shard_map/ppermute | solution.py:20
  321.9 16.8 %collective-permute-start.12 = (bf16[4,128,128]{2,1,0:T(8,128)(2,1)S(1)}, bf16[4,128,128]{2,1,0:T(8,128)(2,1)S(1)}, u32[]{:S(2)}, u32[]{:S(2)}) collective-permute-start(bf16[4,128,128]{2,1,0:T(8,128)(2,1)S(1)} %broadcast_select_fusion.6), channel_id=1, source_target_pairs={{0,896},{32,928},{64,960},{96,992},{128,0},{160,32},{192,64},{224,... | collective-permute-start | bytes 393224 | tf_op jit(solution)/shard_map/ppermute | solution.py:20
  336.7 19.6 %collective-permute-start.17 = (bf16[4,128,128]{2,1,0:T(8,128)(2,1)S(1)}, bf16[4,128,128]{2,1,0:T(8,128)(2,1)S(1)}, u32[]{:S(2)}, u32[]{:S(2)}) collective-permute-start(bf16[4,128,128]{2,1,0:T(8,128)(2,1)S(1)} %broadcast_select_fusion.1), channel_id=1, source_target_pairs={{0,28},{1,29},{2,30},{3,31},{4,0},{5,1},{6,2},{7,3},{8,4},{9,5},{1... | collective-permute-start | bytes 393224 | tf_op jit(solution)/shard_map/ppermute | solution.py:20
  338.7 34.4 %collective-permute-start.13 = (bf16[4,128,128]{2,1,0:T(8,128)(2,1)S(1)}, bf16[4,128,128]{2,1,0:T(8,128)(2,1)S(1)}, u32[]{:S(2)}, u32[]{:S(2)}) collective-permute-start(bf16[4,128,128]{2,1,0:T(8,128)(2,1)S(1)} %broadcast_select_fusion.7), channel_id=1, source_target_pairs={{0,768},{32,800},{64,832},{96,864},{128,896},{160,928},{192,960},{... | collective-permute-start | bytes 393224 | tf_op jit(solution)/shard_map/ppermute | solution.py:20
  356.4 33.7 %collective-permute-start.18 = (bf16[4,128,128]{2,1,0:T(8,128)(2,1)S(1)}, bf16[4,128,128]{2,1,0:T(8,128)(2,1)S(1)}, u32[]{:S(2)}, u32[]{:S(2)}) collective-permute-start(bf16[4,128,128]{2,1,0:T(8,128)(2,1)S(1)} %broadcast_select_fusion.2), channel_id=1, source_target_pairs={{0,24},{1,25},{2,26},{3,27},{4,28},{5,29},{6,30},{7,31},{8,0},{9,1... | collective-permute-start | bytes 393224 | tf_op jit(solution)/shard_map/ppermute | solution.py:20
  373.1 30.9 %collective-permute-start.14 = (bf16[4,128,128]{2,1,0:T(8,128)(2,1)S(1)}, bf16[4,128,128]{2,1,0:T(8,128)(2,1)S(1)}, u32[]{:S(2)}, u32[]{:S(2)}) collective-permute-start(bf16[4,128,128]{2,1,0:T(8,128)(2,1)S(1)} %broadcast_select_fusion.8), channel_id=1, source_target_pairs={{0,512},{32,544},{64,576},{96,608},{128,640},{160,672},{192,704},{... | collective-permute-start | bytes 393224 | tf_op jit(solution)/shard_map/ppermute | solution.py:20
  390.1 56.8 %collective-permute-start.19 = (bf16[4,128,128]{2,1,0:T(8,128)(2,1)S(1)}, bf16[4,128,128]{2,1,0:T(8,128)(2,1)S(1)}, u32[]{:S(2)}, u32[]{:S(2)}) collective-permute-start(bf16[4,128,128]{2,1,0:T(8,128)(2,1)S(1)} %broadcast_select_fusion.3), channel_id=1, source_target_pairs={{0,16},{1,17},{2,18},{3,19},{4,20},{5,21},{6,22},{7,23},{8,24},{9,... | collective-permute-start | bytes 393224 | tf_op jit(solution)/shard_map/ppermute | solution.py:20
  404.1 50.9 %collective-permute-start.32 = (bf16[4,128,128]{2,1,0:T(8,128)(2,1)S(1)}, bf16[4,128,128]{2,1,0:T(8,128)(2,1)S(1)}, u32[]{:S(2)}, u32[]{:S(2)}) collective-permute-start(bf16[4,128,128]{2,1,0:T(8,128)(2,1)S(1)} %broadcast_select_fusion.9), channel_id=1, source_target_pairs={{0,992},{32,0},{64,32},{96,64},{128,96},{160,128},{192,160},{224,1... | collective-permute-start | bytes 393224 | tf_op jit(solution)/shard_map/ppermute | solution.py:20
  459.3 19.7 %collective-permute-start.38 = (bf16[4,128,128]{2,1,0:T(8,128)(2,1)S(1)}, bf16[4,128,128]{2,1,0:T(8,128)(2,1)S(1)}, u32[]{:S(2)}, u32[]{:S(2)}) collective-permute-start(bf16[4,128,128]{2,1,0:T(8,128)(2,1)S(1)} %collective-permute-done.32), channel_id=1, source_target_pairs={{0,992},{32,0},{64,32},{96,64},{128,96},{160,128},{192,160},{224,1... | collective-permute-start | bytes 393224 | tf_op jit(solution)/shard_map/ppermute | solution.py:20
  482.6 19.7 %collective-permute-start.44 = (bf16[4,128,128]{2,1,0:T(8,128)(2,1)S(1)}, bf16[4,128,128]{2,1,0:T(8,128)(2,1)S(1)}, u32[]{:S(2)}, u32[]{:S(2)}) collective-permute-start(bf16[4,128,128]{2,1,0:T(8,128)(2,1)S(1)} %collective-permute-done.38), channel_id=1, source_target_pairs={{0,992},{32,0},{64,32},{96,64},{128,96},{160,128},{192,160},{224,1... | collective-permute-start | bytes 393224 | tf_op jit(solution)/shard_map/ppermute | solution.py:20
  (47 other events, 917.0 us)
where the time goes:
time: 513 us; the launch traced here: 511 us
  starting transfers between devices  401 us (78%)
  waiting for transfers between devices  67.2 us (13%)
  matrix products  21 us (4%)
  between operations  8.57 us (2%)
  local copies, waits for them, and re-layouts  7.26 us (1%)
  other arithmetic  6.82 us (1%)
    ppermute x48, starting transfers between devices, from_behind(): return lax.ppermute(value, axis, pairs)  401 us
    ppermute x48, waiting for transfers between devices, from_behind(): return lax.ppermute(value, axis, pairs)  67.2 us
  transfers between devices with their start and end apart: 48, of which 19 were waited for; matrix products, arithmetic and copies ran while one was open for 3% of the time, Pallas kernels for 0%

commit v1 on v0

v1 whole, which is shorter than its diff:
```python
import jax
import jax.numpy as jnp
from jax import lax
from jax.experimental import pallas as pl
from jax.experimental.pallas import tpu as pltpu
from jax.sharding import PartitionSpec as P

MESH = pl.DeviceIdType.MESH
STEPS = 4
NB = 4
BR = 4
BW = 128
DEAD = NB


class Place:
    def __init__(self):
        self.i = i = lax.axis_index("row")
        self.j = j = lax.axis_index("col")
        self.w, self.x = w, x = j // 4, j % 4
        self.zh, self.pos = zh, pos = i // 8, i % 8

        ahead = i - x
        d1, d2 = (ahead + 3) // 4, (ahead + 6) // 4
        self.two = two = d1 != d2
        self.ha = (x - i + 32) % 4
        self.z1, self.z2 = z1, z2 = (w + d1) % 8, (w + d2) % 8
        g1, g2 = (w - d1 + 16) % 8, (w - d2 + 16) % 8
        self.g1, self.g2 = g1, g2
        need1, need2 = g1 != w, two & (g2 != w)
        self.send1 = need1 & ~(need2 & (g1 > w))
        self.send2 = need2 & ~(need1 & (g1 < w) & (g1 > 0))
        self.own1, self.own2 = z1 == w, two & (z2 == w)
        self.in1 = (z1 != w) & ~(two & (w > z1) & (w - 1 != z1))
        self.in2 = two & (z2 != w) & ~((w + 1 <= 7) & (w + 1 < z2))
        self.late1 = (z1 != w) & ~self.in1
        self.late2 = two & (z2 != w) & ~self.in2
        self.relay1 = two & (w >= 1) & (w < z1)
        self.relay2 = two & (w <= 6) & (w > z2)

        e = j - pos
        self.hb = (pos - j + 32) % 8
        minus = ((e >= -2) & (e <= 11)) | (e >= 30)
        plus = (e >= 12) & (e <= 24)
        self.hop1 = minus | plus
        self.hop2 = (e >= 6) & (e <= 16)
        self.b_to = ((zh + jnp.where(minus, 3, 1)) % 4) * 8 + pos
        self.b_from = ((zh + jnp.where(minus, 1, 3)) % 4) * 8 + pos
        self.first = jnp.where((e <= 0) | (e >= 25), 0, jnp.where((e >= 9) & (e <= 16), 2, 1))
        self.second = jnp.where(
            (e <= -3) | ((e >= 22) & (e <= 29)), 0, jnp.where((e >= 6) & (e <= 13), 2, 1)
        )

    def a_peer(self, turn):
        xd = (self.x + turn) % 4
        step = (self.x - self.i - xd + 64) % 4
        slot = jnp.where(xd <= self.ha, 0, 1)
        return (self.i, self.w * 4 + xd), step, slot

    def a_step_from(self, turn):
        return ((self.x + turn) - self.i - self.x + 64) % 4

    def b_peer(self, step):
        pd = (self.pos - self.j - step + 64) % 8
        slot = jnp.where(step <= self.hb, self.first, self.second)
        return (self.zh * 8 + pd, self.j), pd == self.pos, slot

    def b_source(self, step):
        ps = (self.pos + self.j + step) % 8
        return (self.zh * 8 + ps, self.j)

    def z_peer(self, z):
        return (self.i, z * 4 + self.x)


def live_table(coord, count):
    lane = lax.broadcasted_iota(jnp.int32, (8, 128), 1)
    table = jnp.full((8, 128), DEAD, jnp.int32)
    for s in range(NB):
        live = s < count[0, 0]
        table = jnp.where((lane == coord[0, s]) & live, s, table)
        table = jnp.where(lane == 16 + s, jnp.where(live, coord[0, s], -1), table)
    return table


def move_kernel(
    a_ref, b_ref, a_coord, a_count, b_coord, b_count,
    a_out, b_out, a_table_out, b_table_out,
    a_buf, b_buf, a_own_table, b_own_table, a_table, b_table,
    a_send, a_relay, a_fan, b_send, b_relay, b_fan,
    a_have, b_have, a_got, b_got,
):
    at = Place()
    i, w = at.i, at.w

    a_own_table[...] = live_table(a_coord, a_count)
    b_own_table[...] = live_table(b_coord, b_count)

    def a_own(p):
        return a_own_table if p is NB else a_ref.at[p]

    def b_own(p):
        return b_own_table if p is NB else b_ref.at[p]

    def a_slot(k, p):
        return a_table.at[k] if p is NB else a_buf.at[k, p]

    def b_slot(k, p):
        return b_table.at[k] if p is NB else b_buf.at[k, p]

    def a_final(s, p):
        return a_table_out.at[s] if p is NB else a_out.at[s, p]

    def b_final(s, p):
        return b_table_out.at[s] if p is NB else b_out.at[s, p]

    def remote(src, dst, send, recv, to):
        return pltpu.make_async_remote_copy(
            src_ref=src, dst_ref=dst, send_sem=send, recv_sem=recv, device_id=to, device_id_type=MESH
        )

    def a_direct(n, p):
        to = at.z_peer(at.g1 if n == 0 else at.g2)
        return remote(a_own(p), a_slot(n, p), a_send.at[n, p], a_have.at[n, p], to)

    def a_on(n, p):
        to = at.z_peer(at.w - 1 if n == 0 else at.w + 1)
        return remote(a_slot(n, p), a_slot(1 - n, p), a_relay.at[n, p], a_have.at[1 - n, p], to)

    def a_keep(n, p):
        return pltpu.make_async_copy(a_own(p), a_slot(n, p), a_have.at[n, p])

    def a_spread(turn, p):
        to, step, slot = at.a_peer(turn)
        if turn == 0:
            return pltpu.make_async_copy(a_slot(slot, p), a_final(step, p), a_got.at[step, p])
        return remote(a_slot(slot, p), a_final(step, p), a_fan.at[turn - 1, p], a_got.at[step, p], to)

    def b_direct(p):
        return remote(b_own(p), b_slot(1, p), b_send.at[p], b_have.at[1, p], (at.b_to, at.j))

    def b_on(p):
        return remote(b_slot(1, p), b_slot(2, p), b_relay.at[p], b_have.at[2, p], (at.b_to, at.j))

    def b_keep(p):
        return pltpu.make_async_copy(b_own(p), b_slot(0, p), b_have.at[0, p])

    def b_spread(step, p):
        to, _, slot = at.b_peer(step)
        return remote(b_slot(slot, p), b_final(step, p), b_fan.at[step, p], b_got.at[step, p], to)

    def b_spread_here(step, p):
        _, _, slot = at.b_peer(step)
        return pltpu.make_async_copy(b_slot(slot, p), b_final(step, p), b_got.at[step, p])

    barrier = pltpu.get_barrier_semaphore()

    def greet(device):
        pl.semaphore_signal(barrier, inc=1, device_id=device, device_id_type=MESH)

    def greet_if(cond, device):
        @pl.when(cond)
        def _():
            greet(device)

    def each_piece(body):
        body(NB)
        lax.fori_loop(0, NB, lambda p, c: (body(p), c)[1], 0)

    greet_if(at.in1, at.z_peer(at.z1))
    greet_if(at.in2, at.z_peer(at.z2))
    greet_if(at.late1, at.z_peer(at.w - 1))
    greet_if(at.late2, at.z_peer(at.w + 1))
    greet_if(at.hop1, (at.b_from, at.j))
    for turn in (1, 2, 3):
        greet((i, w * 4 + (at.x + turn) % 4))
    away = jnp.int32(0)
    for step in range(STEPS):
        _, here, _ = at.b_peer(step)
        source = at.b_source(step)
        greet_if(source[0] != i, source)
        away = away + jnp.where(here, 0, 1)

    def keep(p):
        @pl.when(at.own1)
        def _():
            a_keep(0, p).start()

        @pl.when(at.own2)
        def _():
            a_keep(1, p).start()

        b_keep(p).start()

    each_piece(keep)

    def one(flag):
        return jnp.where(flag, 1, 0)

    pl.semaphore_wait(
        barrier,
        3 + away + one(at.send1) + one(at.send2) + one(at.relay1) + one(at.relay2) + one(at.hop1),
    )

    def leave(p):
        @pl.when(at.hop1)
        def _():
            b_direct(p).start()

        @pl.when(at.send1)
        def _():
            a_direct(0, p).start()

        @pl.when(at.send2)
        def _():
            a_direct(1, p).start()

    each_piece(leave)

    def spread_a(p, slot_ready):
        for turn in (1, 2, 3, 0):
            _, _, slot = at.a_peer(turn)

            @pl.when(jnp.where(slot == 0, slot_ready[0], slot_ready[1]))
            def _():
                a_spread(turn, p).start()

    def spread_b(p, ready):
        for step in range(STEPS):
            _, here, slot = at.b_peer(step)

            @pl.when(ready(slot) & ~here)
            def _():
                b_spread(step, p).start()

            @pl.when(ready(slot) & here)
            def _():
                b_spread_here(step, p).start()

    early1, early2 = at.in1 | at.own1, at.in2 | at.own2

    def relay(p):
        b_keep(p).wait()

        @pl.when(at.hop1)
        def _():
            b_direct(p).wait_recv()

        @pl.when(at.hop2)
        def _():
            b_on(p).start()

        @pl.when(early1)
        def _():
            a_direct(0, p).wait_recv()

        @pl.when(at.relay1)
        def _():
            a_on(0, p).start()

        @pl.when(early2)
        def _():
            a_direct(1, p).wait_recv()

        @pl.when(at.relay2)
        def _():
            a_on(1, p).start()

        spread_b(p, lambda slot: slot <= 1)
        spread_a(p, (early1, early2))

    each_piece(relay)

    def late(p):
        @pl.when(at.late1)
        def _():
            a_direct(0, p).wait_recv()

        @pl.when(at.late2)
        def _():
            a_direct(1, p).wait_recv()

        spread_a(p, (at.late1, at.late2))

        @pl.when(at.hop2)
        def _():
            b_on(p).wait_recv()

        spread_b(p, lambda slot: slot == 2)

    each_piece(late)

    def finish(p):
        for step in range(STEPS):
            pltpu.make_async_copy(a_final(step, p), a_final(step, p), a_got.at[step, p]).wait()
            pltpu.make_async_copy(b_final(step, p), b_final(step, p), b_got.at[step, p]).wait()
        for turn in (1, 2, 3):
            a_spread(turn, p).wait_send()
        for step in range(STEPS):
            _, here, _ = at.b_peer(step)

            @pl.when(~here)
            def _():
                b_spread(step, p).wait_send()

        for cond, copy in (
            (at.send1, lambda: a_direct(0, p)),
            (at.send2, lambda: a_direct(1, p)),
            (at.relay1, lambda: a_on(0, p)),
            (at.relay2, lambda: a_on(1, p)),
            (at.hop1, lambda: b_direct(p)),
            (at.hop2, lambda: b_on(p)),
        ):

            @pl.when(cond)
            def _():
                copy().wait_send()

    each_piece(finish)


def move(a_blocks, b_blocks, a_coord, a_count, b_coord, b_count):
    pieces = NB + 1
    dma = pltpu.SemaphoreType.DMA
    panel = jax.ShapeDtypeStruct((STEPS, NB, BW, BW), jnp.bfloat16)
    table = jax.ShapeDtypeStruct((STEPS, 8, 128), jnp.int32)
    anywhere = pl.BlockSpec(memory_space=pl.ANY)
    scalars = pl.BlockSpec(memory_space=pltpu.SMEM)
    return pl.pallas_call(
        move_kernel,
        out_shape=[panel, panel, table, table],
        in_specs=[anywhere] * 2 + [scalars] * 4,
        out_specs=[anywhere] * 4,
        scratch_shapes=[
            pltpu.VMEM((2, NB, BW, BW), jnp.bfloat16),
            pltpu.VMEM((3, NB, BW, BW), jnp.bfloat16),
            pltpu.VMEM((8, 128), jnp.int32),
            pltpu.VMEM((8, 128), jnp.int32),
            pltpu.VMEM((2, 8, 128), jnp.int32),
            pltpu.VMEM((3, 8, 128), jnp.int32),
            dma((2, pieces)),
            dma((2, pieces)),
            dma((3, pieces)),
            dma((pieces,)),
            dma((pieces,)),
            dma((STEPS, pieces)),
            dma((2, pieces)),
            dma((3, pieces)),
            dma((STEPS, pieces)),
            dma((STEPS, pieces)),
        ],
        compiler_params=pltpu.CompilerParams(collective_id=0, has_side_effects=True),
    )(a_blocks, b_blocks, a_coord, a_count, b_coord, b_count)


def product_kernel(a_table, b_table, pattern, a_ref, b_ref, out_ref, total):
    total[...] = jnp.zeros_like(total)
    for step in range(STEPS):
        for slot in range(NB):
            code = a_table[step, 0, 16 + slot]

            @pl.when(code >= 0)
            def _():
                r, k = code // BR, code % BR
                blocks = []
                for c in range(BR):
                    which = b_table[step, 0, k * BR + c]
                    block = b_ref[step, jnp.minimum(which, NB - 1)]
                    kept = (which < NB) & (pattern[r, c] > 0)
                    blocks.append(jnp.where(kept, block, jnp.zeros_like(block)))
                row = jnp.concatenate(blocks, axis=1)
                total[r] += jnp.dot(a_ref[step, slot], row, preferred_element_type=jnp.float32)

    out_ref[...] = total[...].reshape(out_ref.shape).astype(out_ref.dtype)


def product(a_panels, b_panels, a_table, b_table, pattern):
    whole = pl.BlockSpec(memory_space=pltpu.VMEM)
    scalars = pl.BlockSpec(memory_space=pltpu.SMEM)
    span = BR * BW
    return pl.pallas_call(
        product_kernel,
        out_shape=jax.ShapeDtypeStruct((span, span), jnp.bfloat16),
        in_specs=[scalars] * 3 + [whole] * 2,
        out_specs=whole,
        scratch_shapes=[pltpu.VMEM((BR, BW, span), jnp.float32)],
    )(a_table, b_table, pattern, a_panels, b_panels)


def per_device(a_blocks, a_coord, a_count, b_blocks, b_coord, b_count, c_pattern):
    moved = move(a_blocks, b_blocks, a_coord, a_count, b_coord, b_count)
    return product(*moved, c_pattern)


def solution(mesh):
    placed = (
        P("row", "col", None),
        P("row", "col"),
        P("row", "col"),
        P("row", "col", None),
        P("row", "col"),
        P("row", "col"),
        P("row", "col"),
    )
    return jax.shard_map(
        per_device, mesh=mesh, in_specs=placed, out_specs=P("row", "col"), check_vma=False
    )
```

time: 513 us -> 64.8 us (0.13)
  the two profiles are of different devices: /device:TPU:68 before, /device:TPU:90 now
where the time goes in v1:
time: 64.8 us; the launch traced here: 64.6 us
  Pallas kernels  63.3 us (98%)
  between operations  1.3 us (2%)
    pallas_call x1, Pallas kernels, move(): pl.pallas_call(move_kernel, out_shape=[panel, panel, table, table], in_sp...  58.5 us
    pallas_call x1, Pallas kernels, product(): pl.pallas_call(product_kernel, out_shape=jax.ShapeDtypeStruct((span, span...  4.8 us

profile of v1, /device:TPU:90, one launch (start us, length us, event | category | flops | bytes accessed | tf_op | source)
XLA Modules:
  0.0 64.6 jit_solution(16250637600064009054)
XLA Ops:
  1.3 58.5 %shard_map.73 = (bf16[4,4,128,128]{3,2,1,0:T(8,128)(2,1)}, bf16[4,4,128,128]{3,2,1,0:T(8,128)(2,1)}, s32[4,8,128]{2,1,0:T(8,128)}, s32[4,8,128]{2,1,0:T(8,128)}) custom-call(bf16[4,128,128]{2,1,0:T(8,128)(2,1)} %a_ref.1, bf16[4,128,128]{2,1,0:T(8,128)(2,1)} %b_ref.1, s32[1,4]{1,0:T(1,128)} %a_coord.1, s32[1,1]{1,0:T(1,128)S(6)} %copy.8.a_count, ...), custom_call_target="tpu_custom_call" | custom-call | tf_op jit(solution)/shard_map/pallas_call | solution.py:329
  59.8 4.8 %shard_map.74 = bf16[512,512]{1,0:T(8,128)(2,1)} custom-call(s32[4,8,128]{2,1,0:T(8,128)} %get-tuple-element.9.a_table, s32[4,8,128]{2,1,0:T(8,128)} %get-tuple-element.10.b_table, s32[4,4]{1,0:T(4,128)} %pattern.1, bf16[4,4,128,128]{3,2,1,0:T(8,128)(2,1)} %get-tuple-element.11.a_ref, bf16[4,4,128,128]{3,2,1,0:T(8,128)(2,1)} %get-tuple-element.12.b_ref), custom_call_target="tpu_custom_call" | custom-call | tf_op jit(solution)/shard_map/pallas_call | solution.py:381

commit v2 on v1

--- a/solution.py
+++ b/solution.py
@@ -11,6 +11,7 @@
 BR = 4
 BW = 128
 DEAD = NB
+NP = 4
 
 
 class Place:
@@ -40,12 +41,21 @@
 
         e = j - pos
         self.hb = (pos - j + 32) % 8
-        minus = ((e >= -2) & (e <= 11)) | (e >= 30)
-        plus = (e >= 12) & (e <= 24)
-        self.hop1 = minus | plus
-        self.hop2 = (e >= 6) & (e <= 16)
-        self.b_to = ((zh + jnp.where(minus, 3, 1)) % 4) * 8 + pos
-        self.b_from = ((zh + jnp.where(minus, 1, 3)) % 4) * 8 + pos
+        self.core, self.twin = pos % 2, (zh * 8 + pos + 1 - 2 * (pos % 2), j)
+        down = ((e >= -2) & (e <= 8)) | (e >= 30)
+        up = (e >= 14) & (e <= 24)
+        self.near = near = down | up
+        self.far = far = (e >= 6) & (e <= 16)
+        self.near_to = jnp.where(down, (zh + 3) % 4, (zh + 1) % 4) * 8 + pos
+        self.near_from = jnp.where(down, (zh + 1) % 4, (zh + 3) % 4) * 8 + pos
+        self.far_to = ((zh + 2) % 4) * 8 + pos
+        late = near & ~far
+        greet_up = near & ((zh <= 1) | ((zh == 2) & ~late))
+        greet_down = near & ((zh == 0) | ((zh == 3) & late))
+        self.greet_to = jnp.where(down, greet_down, greet_up)
+        self.greet_from = jnp.where(down, greet_up, greet_down)
+        self.met_to, self.met_from = near & ~self.greet_to, near & ~self.greet_from
+        self.greet_far, self.met_far = far & (zh <= 1), far & (zh >= 2)
         self.first = jnp.where((e <= 0) | (e >= 25), 0, jnp.where((e >= 9) & (e <= 16), 2, 1))
         self.second = jnp.where(
             (e <= -3) | ((e >= 22) & (e <= 29)), 0, jnp.where((e >= 6) & (e <= 13), 2, 1)
@@ -64,6 +74,9 @@
         pd = (self.pos - self.j - step + 64) % 8
         slot = jnp.where(step <= self.hb, self.first, self.second)
         return (self.zh * 8 + pd, self.j), pd == self.pos, slot
+
+    def b_direct(self, step):
+        return (self.pos - self.j) % 2 == 0 if step == 3 else step != 1
 
     def b_source(self, step):
         ps = (self.pos + self.j + step) % 8
@@ -87,8 +100,8 @@
     a_ref, b_ref, a_coord, a_count, b_coord, b_count,
     a_out, b_out, a_table_out, b_table_out,
     a_buf, b_buf, a_own_table, b_own_table, a_table, b_table,
-    a_send, a_relay, a_fan, b_send, b_relay, b_fan,
-    a_have, b_have, a_got, b_got,
+    a_send, a_relay, a_fan, b_send, b_fan, b_pass,
+    a_have, b_have, a_got, b_got, near_ready, far_ready, below, above,
 ):
     at = Place()
     i, w = at.i, at.w
@@ -96,23 +109,26 @@
     a_own_table[...] = live_table(a_coord, a_count)
     b_own_table[...] = live_table(b_coord, b_count)
 
+    def part(p):
+        return pl.ds(p * (NB // NP), NB // NP)
+
     def a_own(p):
-        return a_own_table if p is NB else a_ref.at[p]
+        return a_own_table if p is NB else a_ref.at[part(p)]
 
     def b_own(p):
-        return b_own_table if p is NB else b_ref.at[p]
+        return b_own_table if p is NB else b_ref.at[part(p)]
 
     def a_slot(k, p):
-        return a_table.at[k] if p is NB else a_buf.at[k, p]
+        return a_table.at[k] if p is NB else a_buf.at[k, part(p)]
 
     def b_slot(k, p):
-        return b_table.at[k] if p is NB else b_buf.at[k, p]
+        return b_table.at[k] if p is NB else b_buf.at[k, part(p)]
 
     def a_final(s, p):
-        return a_table_out.at[s] if p is NB else a_out.at[s, p]
+        return a_table_out.at[s] if p is NB else a_out.at[s, part(p)]
 
     def b_final(s, p):
-        return b_table_out.at[s] if p is NB else b_out.at[s, p]
+        return b_table_out.at[s] if p is NB else b_out.at[s, part(p)]
 
     def remote(src, dst, send, recv, to):
         return pltpu.make_async_remote_copy(
@@ -136,11 +152,11 @@
             return pltpu.make_async_copy(a_slot(slot, p), a_final(step, p), a_got.at[step, p])
         return remote(a_slot(slot, p), a_final(step, p), a_fan.at[turn - 1, p], a_got.at[step, p], to)
 
-    def b_direct(p):
-        return remote(b_own(p), b_slot(1, p), b_send.at[p], b_have.at[1, p], (at.b_to, at.j))
-
-    def b_on(p):
-        return remote(b_slot(1, p), b_slot(2, p), b_relay.at[p], b_have.at[2, p], (at.b_to, at.j))
+    def b_near(p):
+        return remote(b_own(p), b_slot(1, p), b_send.at[0, p], b_have.at[1, p], (at.near_to, at.j))
+
+    def b_far(p):
+        return remote(b_own(p), b_slot(2, p), b_send.at[1, p], b_have.at[2, p], (at.far_to, at.j))
 
     def b_keep(p):
         return pltpu.make_async_copy(b_own(p), b_slot(0, p), b_have.at[0, p])
@@ -153,6 +169,12 @@
         _, _, slot = at.b_peer(step)
         return pltpu.make_async_copy(b_slot(slot, p), b_final(step, p), b_got.at[step, p])
 
+    def b_twin(step, to, p):
+        return remote(b_final(step, p), b_final(to, p), b_pass.at[to // 2, p], b_got.at[to, p], at.twin)
+
+    def b_wait(step, p):
+        pltpu.make_async_copy(b_final(step, p), b_final(step, p), b_got.at[step, p]).wait()
+
     barrier = pltpu.get_barrier_semaphore()
 
     def greet(device):
@@ -165,21 +187,22 @@
 
     def each_piece(body):
         body(NB)
-        lax.fori_loop(0, NB, lambda p, c: (body(p), c)[1], 0)
-
-    greet_if(at.in1, at.z_peer(at.z1))
-    greet_if(at.in2, at.z_peer(at.z2))
-    greet_if(at.late1, at.z_peer(at.w - 1))
-    greet_if(at.late2, at.z_peer(at.w + 1))
-    greet_if(at.hop1, (at.b_from, at.j))
+        lax.fori_loop(0, NP, lambda p, c: (body(p), c)[1], 0)
+
+    greet_if(w > 0, at.z_peer(w - 1))
+    greet_if(w < 7, at.z_peer(w + 1))
+    greet_if(at.greet_to, (at.near_to, at.j))
+    greet_if(at.greet_from, (at.near_from, at.j))
+    greet_if(at.greet_far, (at.far_to, at.j))
     for turn in (1, 2, 3):
         greet((i, w * 4 + (at.x + turn) % 4))
-    away = jnp.int32(0)
-    for step in range(STEPS):
+    greet(at.twin)
+    away = jnp.int32(1)
+    for step in (0, 2, 3):
         _, here, _ = at.b_peer(step)
         source = at.b_source(step)
-        greet_if(source[0] != i, source)
-        away = away + jnp.where(here, 0, 1)
+        greet_if((source[0] != i) & ((at.core == 1) | (step != 3)), source)
+        away = away + jnp.where(at.b_direct(step) & ~here, 1, 0)
 
     def keep(p):
         @pl.when(at.own1)
@@ -199,14 +222,16 @@
 
     pl.semaphore_wait(
         barrier,
-        3 + away + one(at.send1) + one(at.send2) + one(at.relay1) + one(at.relay2) + one(at.hop1),
+        3 + away + one(w > 0) + one(w < 7) + one(at.met_to) + one(at.met_from) + one(at.met_far),
     )
 
-    def leave(p):
-        @pl.when(at.hop1)
-        def _():
-            b_direct(p).start()
-
+    def leave_near(p):
+        b_near(p).start()
+
+    def leave_far(p):
+        b_far(p).start()
+
+    def leave_a(p):
         @pl.when(at.send1)
         def _():
             a_direct(0, p).start()
@@ -214,8 +239,6 @@
         @pl.when(at.send2)
         def _():
             a_direct(1, p).start()
-
-    each_piece(leave)
 
     def spread_a(p, slot_ready):
         for turn in (1, 2, 3, 0):
@@ -226,30 +249,30 @@
                 a_spread(turn, p).start()
 
     def spread_b(p, ready):
-        for step in range(STEPS):
+        for step in (0, 2, 3):
             _, here, slot = at.b_peer(step)
-
-            @pl.when(ready(slot) & ~here)
+            mine = ready(slot) & at.b_direct(step)
+
+            @pl.when(mine & ~here)
             def _():
                 b_spread(step, p).start()
 
-            @pl.when(ready(slot) & here)
+            @pl.when(mine & here)
             def _():
                 b_spread_here(step, p).start()
 
     early1, early2 = at.in1 | at.own1, at.in2 | at.own2
 
-    def relay(p):
+    def near_b(p):
         b_keep(p).wait()
 
-        @pl.when(at.hop1)
-        def _():
-            b_direct(p).wait_recv()
-
-        @pl.when(at.hop2)
-        def _():
-            b_on(p).start()
-
+        @pl.when(at.near)
+        def _():
+            b_near(p).wait_recv()
+
+        spread_b(p, lambda slot: slot <= 1)
+
+    def relay_a(p):
         @pl.when(early1)
         def _():
             a_direct(0, p).wait_recv()
@@ -266,12 +289,9 @@
         def _():
             a_on(1, p).start()
 
-        spread_b(p, lambda slot: slot <= 1)
         spread_a(p, (early1, early2))
 
-    each_piece(relay)
-
-    def late(p):
+    def late_a(p):
         @pl.when(at.late1)
         def _():
             a_direct(0, p).wait_recv()
@@ -282,24 +302,124 @@
 
         spread_a(p, (at.late1, at.late2))
 
-        @pl.when(at.hop2)
-        def _():
-            b_on(p).wait_recv()
+    def far_b(p):
+        @pl.when(at.far)
+        def _():
+            b_far(p).wait_recv()
 
         spread_b(p, lambda slot: slot == 2)
 
-    each_piece(late)
+    @pl.when(at.met_from)
+    def _():
+        pl.semaphore_signal(near_ready, inc=1, device_id=(at.near_from, at.j), device_id_type=MESH)
+
+    @pl.when(at.met_far)
+    def _():
+        pl.semaphore_signal(far_ready, inc=1, device_id=(at.far_to, at.j), device_id_type=MESH)
+
+    @pl.when(at.met_far & (at.zh == 2))
+    def _():
+        each_piece(leave_far)
+
+    @pl.when(at.met_to)
+    def _():
+        each_piece(leave_near)
+
+    @pl.when(at.met_far & (at.zh == 3))
+    def _():
+        each_piece(leave_far)
+
+    def from_below():
+        @pl.when(w > 0)
+        def _():
+            pl.semaphore_wait(below, 1)
+
+        @pl.when(w < 7)
+        def _():
+            pl.semaphore_signal(below, inc=1, device_id=at.z_peer(w + 1), device_id_type=MESH)
+
+    def from_above():
+        @pl.when(w < 7)
+        def _():
+            pl.semaphore_wait(above, 1)
+
+        @pl.when(w > 0)
+        def _():
+            pl.semaphore_signal(above, inc=1, device_id=at.z_peer(w - 1), device_id_type=MESH)
+
+    @pl.when(w < 4)
+    def _():
+        from_below()
+        from_above()
+
+    @pl.when(w >= 4)
+    def _():
+        from_above()
+        from_below()
+
+    each_piece(leave_a)
+    a_first = at.zh == 0
+
+    @pl.when(a_first)
+    def _():
+        each_piece(relay_a)
+        each_piece(late_a)
+
+    @pl.when(at.greet_to)
+    def _():
+        pl.semaphore_wait(near_ready, 1)
+        each_piece(leave_near)
+
+    @pl.when(at.greet_far)
+    def _():
+        pl.semaphore_wait(far_ready, 1)
+        each_piece(leave_far)
+
+    each_piece(near_b)
+
+    @pl.when(~a_first)
+    def _():
+        each_piece(relay_a)
+        each_piece(late_a)
+
+    each_piece(far_b)
+
+    def share(p):
+        b_wait(0, p)
+
+        @pl.when(at.core == 1)
+        def _():
+            b_twin(0, 1, p).start()
+
+        b_wait(2, p)
+
+        @pl.when(at.core == 1)
+        def _():
+            b_twin(2, 3, p).start()
+
+        @pl.when(at.core == 0)
+        def _():
+            b_twin(2, 1, p).start()
+
+    each_piece(share)
 
     def finish(p):
         for step in range(STEPS):
             pltpu.make_async_copy(a_final(step, p), a_final(step, p), a_got.at[step, p]).wait()
-            pltpu.make_async_copy(b_final(step, p), b_final(step, p), b_got.at[step, p]).wait()
+        b_wait(1, p)
+        b_wait(3, p)
+        b_twin(0, 1, p).wait_send()
+
+        @pl.when(at.core == 1)
+        def _():
+            b_twin(2, 3, p).wait_send()
+
         for turn in (1, 2, 3):
             a_spread(turn, p).wait_send()
-        for step in range(STEPS):
+        for step in (0, 2, 3):
             _, here, _ = at.b_peer(step)
 
-            @pl.when(~here)
+            @pl.when(at.b_direct(step) & ~here)
             def _():
                 b_spread(step, p).wait_send()
 
@@ -308,8 +428,8 @@
             (at.send2, lambda: a_direct(1, p)),
             (at.relay1, lambda: a_on(0, p)),
             (at.relay2, lambda: a_on(1, p)),
-            (at.hop1, lambda: b_direct(p)),
-            (at.hop2, lambda: b_on(p)),
+            (at.near, lambda: b_near(p)),
+            (at.far, lambda: b_far(p)),
         ):
 
             @pl.when(cond)
@@ -341,13 +461,17 @@
             dma((2, pieces)),
             dma((2, pieces)),
             dma((3, pieces)),
-            dma((pieces,)),
-            dma((pieces,)),
+            dma((2, pieces)),
             dma((STEPS, pieces)),
+            dma((2, pieces)),
             dma((2, pieces)),
             dma((3, pieces)),
             dma((STEPS, pieces)),
             dma((STEPS, pieces)),
+            pltpu.SemaphoreType.REGULAR,
+            pltpu.SemaphoreType.REGULAR,
+            pltpu.SemaphoreType.REGULAR,
+            pltpu.SemaphoreType.REGULAR,
         ],
         compiler_params=pltpu.CompilerParams(collective_id=0, has_side_effects=True),
     )(a_blocks, b_blocks, a_coord, a_count, b_coord, b_count)

time: 64.8 us -> 61.6 us (0.951)
  the two profiles are of different devices: /device:TPU:90 before, /device:TPU:903 now
where the time goes in v2:
time: 61.6 us; the launch traced here: 61.4 us
  Pallas kernels  60.1 us (98%)
  between operations  1.3 us (2%)
    pallas_call x1, Pallas kernels, move(): pl.pallas_call(move_kernel, out_shape=[panel, panel, table, table], in_sp...  56.6 us
    pallas_call x1, Pallas kernels, product(): pl.pallas_call(product_kernel, out_shape=jax.ShapeDtypeStruct((span, span...  3.44 us

profile of v2, /device:TPU:903, one launch (start us, length us, event | category | flops | bytes accessed | tf_op | source)
XLA Modules:
  0.0 61.4 jit_solution(6167497556107195590)
XLA Ops:
  1.3 56.6 %shard_map.73 = (bf16[4,4,128,128]{3,2,1,0:T(8,128)(2,1)}, bf16[4,4,128,128]{3,2,1,0:T(8,128)(2,1)}, s32[4,8,128]{2,1,0:T(8,128)}, s32[4,8,128]{2,1,0:T(8,128)}) custom-call(bf16[4,128,128]{2,1,0:T(8,128)(2,1)} %a_ref.1, bf16[4,128,128]{2,1,0:T(8,128)(2,1)} %b_ref.1, s32[1,4]{1,0:T(1,128)} %a_coord.1, s32[1,1]{1,0:T(1,128)S(6)} %copy.8.a_count, ...), custom_call_target="tpu_custom_call" | custom-call | tf_op jit(solution)/shard_map/pallas_call | solution.py:449
  57.9 3.4 %shard_map.74 = bf16[512,512]{1,0:T(8,128)(2,1)} custom-call(s32[4,8,128]{2,1,0:T(8,128)} %get-tuple-element.9.a_table, s32[4,8,128]{2,1,0:T(8,128)} %get-tuple-element.10.b_table, s32[4,4]{1,0:T(4,128)} %pattern.1, bf16[4,4,128,128]{3,2,1,0:T(8,128)(2,1)} %get-tuple-element.11.a_ref, bf16[4,4,128,128]{3,2,1,0:T(8,128)(2,1)} %get-tuple-element.12.b_ref), custom_call_target="tpu_custom_call" | custom-call | tf_op jit(solution)/shard_map/pallas_call | solution.py:505

commit v3 on v2

--- a/solution.py
+++ b/solution.py
@@ -49,13 +49,22 @@
         self.near_to = jnp.where(down, (zh + 3) % 4, (zh + 1) % 4) * 8 + pos
         self.near_from = jnp.where(down, (zh + 1) % 4, (zh + 3) % 4) * 8 + pos
         self.far_to = ((zh + 2) % 4) * 8 + pos
-        late = near & ~far
+        late = up & ~far
         greet_up = near & ((zh <= 1) | ((zh == 2) & ~late))
         greet_down = near & ((zh == 0) | ((zh == 3) & late))
         self.greet_to = jnp.where(down, greet_down, greet_up)
         self.greet_from = jnp.where(down, greet_up, greet_down)
         self.met_to, self.met_from = near & ~self.greet_to, near & ~self.greet_from
-        self.greet_far, self.met_far = far & (zh <= 1), far & (zh >= 2)
+        self.far_send = far & (~near | (zh == 2))
+        self.pass_on = near & far & (self.near_from // 8 != 2)
+        alone = far & ~near
+        self.far_send = self.far_send & ~(alone & (zh == 1))
+        self.swap_send, self.swap_get = alone & (zh == 1), alone & (zh == 0)
+        self.swap_to, self.swap_on = (1 - zh) * 8 + pos, 24 + pos
+        self.swap_end = alone & (zh == 3)
+        self.greet_far = far & ((zh == 0) | ((zh == 1) & ~near))
+        self.met_far = far & ((zh == 2) | ((zh == 3) & ~near))
+        self.told_far, self.tell_far = alone & (zh == 0), alone & (zh == 2)
         self.first = jnp.where((e <= 0) | (e >= 25), 0, jnp.where((e >= 9) & (e <= 16), 2, 1))
         self.second = jnp.where(
             (e <= -3) | ((e >= 22) & (e <= 29)), 0, jnp.where((e >= 6) & (e <= 13), 2, 1)
@@ -87,8 +96,8 @@
 
 
 def live_table(coord, count):
-    lane = lax.broadcasted_iota(jnp.int32, (8, 128), 1)
-    table = jnp.full((8, 128), DEAD, jnp.int32)
+    lane = lax.broadcasted_iota(jnp.int32, (1, 128), 1)
+    table = jnp.full((1, 128), DEAD, jnp.int32)
     for s in range(NB):
         live = s < count[0, 0]
         table = jnp.where((lane == coord[0, s]) & live, s, table)
@@ -100,8 +109,8 @@
     a_ref, b_ref, a_coord, a_count, b_coord, b_count,
     a_out, b_out, a_table_out, b_table_out,
     a_buf, b_buf, a_own_table, b_own_table, a_table, b_table,
-    a_send, a_relay, a_fan, b_send, b_fan, b_pass,
-    a_have, b_have, a_got, b_got, near_ready, far_ready, below, above,
+    a_send, a_relay, a_fan, b_send, b_fan, b_twins,
+    a_have, b_have, a_got, b_got, near_ready, far_ready, swap_ready, below, above,
 ):
     at = Place()
     i, w = at.i, at.w
@@ -158,6 +167,15 @@
     def b_far(p):
         return remote(b_own(p), b_slot(2, p), b_send.at[1, p], b_have.at[2, p], (at.far_to, at.j))
 
+    def b_pass(p):
+        return remote(b_slot(1, p), b_slot(2, p), b_send.at[2, p], b_have.at[2, p], (at.near_to, at.j))
+
+    def b_swap(p):
+        return remote(b_own(p), b_slot(3, p), b_send.at[1, p], b_have.at[3, p], (at.swap_to, at.j))
+
+    def b_swap_on(p):
+        return remote(b_slot(3, p), b_slot(2, p), b_send.at[2, p], b_have.at[2, p], (at.swap_on, at.j))
+
     def b_keep(p):
         return pltpu.make_async_copy(b_own(p), b_slot(0, p), b_have.at[0, p])
 
@@ -170,7 +188,7 @@
         return pltpu.make_async_copy(b_slot(slot, p), b_final(step, p), b_got.at[step, p])
 
     def b_twin(step, to, p):
-        return remote(b_final(step, p), b_final(to, p), b_pass.at[to // 2, p], b_got.at[to, p], at.twin)
+        return remote(b_final(step, p), b_final(to, p), b_twins.at[to // 2, p], b_got.at[to, p], at.twin)
 
     def b_wait(step, p):
         pltpu.make_async_copy(b_final(step, p), b_final(step, p), b_got.at[step, p]).wait()
@@ -194,6 +212,8 @@
     greet_if(at.greet_to, (at.near_to, at.j))
     greet_if(at.greet_from, (at.near_from, at.j))
     greet_if(at.greet_far, (at.far_to, at.j))
+    greet_if(at.swap_get, (at.swap_to, at.j))
+    greet_if(at.swap_get, (at.swap_on, at.j))
     for turn in (1, 2, 3):
         greet((i, w * 4 + (at.x + turn) % 4))
     greet(at.twin)
@@ -222,7 +242,7 @@
 
     pl.semaphore_wait(
         barrier,
-        3 + away + one(w > 0) + one(w < 7) + one(at.met_to) + one(at.met_from) + one(at.met_far),
+        3 + away + one(w > 0) + one(w < 7) + one(at.met_to) + one(at.met_from) + one(at.met_far) + one(at.swap_send) + one(at.swap_end),
     )
 
     def leave_near(p):
@@ -270,6 +290,10 @@
         def _():
             b_near(p).wait_recv()
 
+        @pl.when(at.pass_on)
+        def _():
+            b_pass(p).start()
+
         spread_b(p, lambda slot: slot <= 1)
 
     def relay_a(p):
@@ -313,11 +337,15 @@
     def _():
         pl.semaphore_signal(near_ready, inc=1, device_id=(at.near_from, at.j), device_id_type=MESH)
 
-    @pl.when(at.met_far)
+    @pl.when(at.swap_end)
+    def _():
+        pl.semaphore_signal(swap_ready, inc=1, device_id=(at.pos, at.j), device_id_type=MESH)
+
+    @pl.when(at.tell_far)
     def _():
         pl.semaphore_signal(far_ready, inc=1, device_id=(at.far_to, at.j), device_id_type=MESH)
 
-    @pl.when(at.met_far & (at.zh == 2))
+    @pl.when(at.far_send & (at.zh == 2))
     def _():
         each_piece(leave_far)
 
@@ -325,7 +353,14 @@
     def _():
         each_piece(leave_near)
 
-    @pl.when(at.met_far & (at.zh == 3))
+    def leave_swap(p):
+        b_swap(p).start()
+
+    @pl.when(at.swap_send)
+    def _():
+        each_piece(leave_swap)
+
+    @pl.when(at.far_send & (at.zh == 3))
     def _():
         each_piece(leave_far)
 
@@ -370,7 +405,16 @@
         pl.semaphore_wait(near_ready, 1)
         each_piece(leave_near)
 
-    @pl.when(at.greet_far)
+    def swap_on(p):
+        b_swap(p).wait_recv()
+        b_swap_on(p).start()
+
+    @pl.when(at.swap_get)
+    def _():
+        pl.semaphore_wait(swap_ready, 1)
+        each_piece(swap_on)
+
+    @pl.when(at.told_far)
     def _():
         pl.semaphore_wait(far_ready, 1)
         each_piece(leave_far)
@@ -429,7 +473,10 @@
             (at.relay1, lambda: a_on(0, p)),
             (at.relay2, lambda: a_on(1, p)),
             (at.near, lambda: b_near(p)),
-            (at.far, lambda: b_far(p)),
+            (at.far_send, lambda: b_far(p)),
+            (at.pass_on, lambda: b_pass(p)),
+            (at.swap_send, lambda: b_swap(p)),
+            (at.swap_get, lambda: b_swap_on(p)),
         ):
 
             @pl.when(cond)
@@ -443,7 +490,7 @@
     pieces = NB + 1
     dma = pltpu.SemaphoreType.DMA
     panel = jax.ShapeDtypeStruct((STEPS, NB, BW, BW), jnp.bfloat16)
-    table = jax.ShapeDtypeStruct((STEPS, 8, 128), jnp.int32)
+    table = jax.ShapeDtypeStruct((STEPS, 1, 128), jnp.int32)
     anywhere = pl.BlockSpec(memory_space=pl.ANY)
     scalars = pl.BlockSpec(memory_space=pltpu.SMEM)
     return pl.pallas_call(
@@ -453,21 +500,22 @@
         out_specs=[anywhere] * 4,
         scratch_shapes=[
             pltpu.VMEM((2, NB, BW, BW), jnp.bfloat16),
-            pltpu.VMEM((3, NB, BW, BW), jnp.bfloat16),
-            pltpu.VMEM((8, 128), jnp.int32),
-            pltpu.VMEM((8, 128), jnp.int32),
-            pltpu.VMEM((2, 8, 128), jnp.int32),
-            pltpu.VMEM((3, 8, 128), jnp.int32),
+            pltpu.VMEM((4, NB, BW, BW), jnp.bfloat16),
+            pltpu.VMEM((1, 128), jnp.int32),
+            pltpu.VMEM((1, 128), jnp.int32),
+            pltpu.VMEM((2, 1, 128), jnp.int32),
+            pltpu.VMEM((4, 1, 128), jnp.int32),
             dma((2, pieces)),
             dma((2, pieces)),
             dma((3, pieces)),
-            dma((2, pieces)),
+            dma((3, pieces)),
             dma((STEPS, pieces)),
             dma((2, pieces)),
             dma((2, pieces)),
-            dma((3, pieces)),
+            dma((4, pieces)),
             dma((STEPS, pieces)),
             dma((STEPS, pieces)),
+            pltpu.SemaphoreType.REGULAR,
             pltpu.SemaphoreType.REGULAR,
             pltpu.SemaphoreType.REGULAR,
             pltpu.SemaphoreType.REGULAR,
@@ -482,16 +530,16 @@
     for step in range(STEPS):
         for slot in range(NB):
             code = a_table[step, 0, 16 + slot]
-
-            @pl.when(code >= 0)
+            r, k = jnp.maximum(code, 0) // BR, jnp.maximum(code, 0) % BR
+            which = [b_table[step, 0, k * BR + c] for c in range(BR)]
+            kept = [(which[c] < NB) & (pattern[r, c] > 0) for c in range(BR)]
+
+            @pl.when((code >= 0) & (kept[0] | kept[1] | kept[2] | kept[3]))
             def _():
-                r, k = code // BR, code % BR
                 blocks = []
                 for c in range(BR):
-                    which = b_table[step, 0, k * BR + c]
-                    block = b_ref[step, jnp.minimum(which, NB - 1)]
-                    kept = (which < NB) & (pattern[r, c] > 0)
-                    blocks.append(jnp.where(kept, block, jnp.zeros_like(block)))
+                    block = b_ref[step, jnp.minimum(which[c], NB - 1)]
+                    blocks.append(jnp.where(kept[c], block, jnp.zeros_like(block)))
                 row = jnp.concatenate(blocks, axis=1)
                 total[r] += jnp.dot(a_ref[step, slot], row, preferred_element_type=jnp.float32)
 

time: 61.6 us -> 58.1 us (0.943)
  the two profiles are of different devices: /device:TPU:903 before, /device:TPU:403 now
where the time goes in v3:
time: 58.1 us; the launch traced here: 57.9 us
  Pallas kernels  56.6 us (97%)
  between operations  1.3 us (2%)
    pallas_call x1, Pallas kernels, move(): pl.pallas_call(move_kernel, out_shape=[panel, panel, table, table], in_sp...  53 us
    pallas_call x1, Pallas kernels, product(): pl.pallas_call(product_kernel, out_shape=jax.ShapeDtypeStruct((span, span...  3.62 us

profile of v3, /device:TPU:403, one launch (start us, length us, event | category | flops | bytes accessed | tf_op | source)
XLA Modules:
  0.0 57.9 jit_solution(4441079719015834863)
XLA Ops:
  1.3 53.0 %shard_map.73 = (bf16[4,4,128,128]{3,2,1,0:T(8,128)(2,1)}, bf16[4,4,128,128]{3,2,1,0:T(8,128)(2,1)}, s32[4,1,128]{2,1,0:T(1,128)}, s32[4,1,128]{2,1,0:T(1,128)}) custom-call(bf16[4,128,128]{2,1,0:T(8,128)(2,1)} %a_ref.1, bf16[4,128,128]{2,1,0:T(8,128)(2,1)} %b_ref.1, s32[1,4]{1,0:T(1,128)} %a_coord.1, s32[1,1]{1,0:T(1,128)S(6)} %copy.8.a_count, ...), custom_call_target="tpu_custom_call" | custom-call | tf_op jit(solution)/shard_map/pallas_call | solution.py:496
  54.3 3.6 %shard_map.74 = bf16[512,512]{1,0:T(8,128)(2,1)} custom-call(s32[4,1,128]{2,1,0:T(1,128)} %get-tuple-element.9.a_table, s32[4,1,128]{2,1,0:T(1,128)} %get-tuple-element.10.b_table, s32[4,4]{1,0:T(4,128)} %pattern.1, bf16[4,4,128,128]{3,2,1,0:T(8,128)(2,1)} %get-tuple-element.11.a_ref, bf16[4,4,128,128]{3,2,1,0:T(8,128)(2,1)} %get-tuple-element.12.b_ref), custom_call_target="tpu_custom_call" | custom-call | tf_op jit(solution)/shard_map/pallas_call | solution.py:553

commit v4 on v3

--- a/solution.py
+++ b/solution.py
@@ -49,14 +49,14 @@
         self.near_to = jnp.where(down, (zh + 3) % 4, (zh + 1) % 4) * 8 + pos
         self.near_from = jnp.where(down, (zh + 1) % 4, (zh + 3) % 4) * 8 + pos
         self.far_to = ((zh + 2) % 4) * 8 + pos
-        late = up & ~far
+        late = up
         greet_up = near & ((zh <= 1) | ((zh == 2) & ~late))
         greet_down = near & ((zh == 0) | ((zh == 3) & late))
         self.greet_to = jnp.where(down, greet_down, greet_up)
         self.greet_from = jnp.where(down, greet_up, greet_down)
         self.met_to, self.met_from = near & ~self.greet_to, near & ~self.greet_from
-        self.far_send = far & (~near | (zh == 2))
-        self.pass_on = near & far & (self.near_from // 8 != 2)
+        self.far_send = far & ~near
+        self.pass_on = near & far
         alone = far & ~near
         self.far_send = self.far_send & ~(alone & (zh == 1))
         self.swap_send, self.swap_get = alone & (zh == 1), alone & (zh == 0)
@@ -115,11 +115,8 @@
     at = Place()
     i, w = at.i, at.w
 
-    a_own_table[...] = live_table(a_coord, a_count)
-    b_own_table[...] = live_table(b_coord, b_count)
-
     def part(p):
-        return pl.ds(p * (NB // NP), NB // NP)
+        return pl.ds(p * (NB // NP), NB // NP) if isinstance(p, (int, jax.Array)) else p
 
     def a_own(p):
         return a_own_table if p is NB else a_ref.at[part(p)]
@@ -144,13 +141,16 @@
             src_ref=src, dst_ref=dst, send_sem=send, recv_sem=recv, device_id=to, device_id_type=MESH
         )
 
+    def whole(p):
+        return 1 if p is NB else 0
+
     def a_direct(n, p):
         to = at.z_peer(at.g1 if n == 0 else at.g2)
-        return remote(a_own(p), a_slot(n, p), a_send.at[n, p], a_have.at[n, p], to)
+        return remote(a_own(p), a_slot(n, p), a_send.at[n, whole(p)], a_have.at[n, p], to)
 
     def a_on(n, p):
         to = at.z_peer(at.w - 1 if n == 0 else at.w + 1)
-        return remote(a_slot(n, p), a_slot(1 - n, p), a_relay.at[n, p], a_have.at[1 - n, p], to)
+        return remote(a_slot(n, p), a_slot(1 - n, p), a_relay.at[n, whole(p)], a_have.at[1 - n, p], to)
 
     def a_keep(n, p):
         return pltpu.make_async_copy(a_own(p), a_slot(n, p), a_have.at[n, p])
@@ -158,40 +158,44 @@
     def a_spread(turn, p):
         to, step, slot = at.a_peer(turn)
         if turn == 0:
-            return pltpu.make_async_copy(a_slot(slot, p), a_final(step, p), a_got.at[step, p])
-        return remote(a_slot(slot, p), a_final(step, p), a_fan.at[turn - 1, p], a_got.at[step, p], to)
+            return pltpu.make_async_copy(a_slot(slot, p), a_final(step, p), a_got.at[step, whole(p)])
+        return remote(a_slot(slot, p), a_final(step, p), a_fan.at[turn - 1, whole(p)], a_got.at[step, whole(p)], to)
 
     def b_near(p):
-        return remote(b_own(p), b_slot(1, p), b_send.at[0, p], b_have.at[1, p], (at.near_to, at.j))
+        return remote(b_own(p), b_slot(1, p), b_send.at[0, whole(p)], b_have.at[1, p], (at.near_to, at.j))
 
     def b_far(p):
-        return remote(b_own(p), b_slot(2, p), b_send.at[1, p], b_have.at[2, p], (at.far_to, at.j))
+        return remote(b_own(p), b_slot(2, p), b_send.at[1, whole(p)], b_have.at[2, p], (at.far_to, at.j))
 
     def b_pass(p):
-        return remote(b_slot(1, p), b_slot(2, p), b_send.at[2, p], b_have.at[2, p], (at.near_to, at.j))
+        return remote(b_slot(1, p), b_slot(2, p), b_send.at[2, whole(p)], b_have.at[2, p], (at.near_to, at.j))
 
     def b_swap(p):
-        return remote(b_own(p), b_slot(3, p), b_send.at[1, p], b_have.at[3, p], (at.swap_to, at.j))
+        return remote(b_own(p), b_slot(3, p), b_send.at[1, whole(p)], b_have.at[3, p], (at.swap_to, at.j))
 
     def b_swap_on(p):
-        return remote(b_slot(3, p), b_slot(2, p), b_send.at[2, p], b_have.at[2, p], (at.swap_on, at.j))
+        return remote(b_slot(3, p), b_slot(2, p), b_send.at[2, whole(p)], b_have.at[2, p], (at.swap_on, at.j))
 
     def b_keep(p):
         return pltpu.make_async_copy(b_own(p), b_slot(0, p), b_have.at[0, p])
 
     def b_spread(step, p):
         to, _, slot = at.b_peer(step)
-        return remote(b_slot(slot, p), b_final(step, p), b_fan.at[step, p], b_got.at[step, p], to)
+        return remote(b_slot(slot, p), b_final(step, p), b_fan.at[step, whole(p)], b_got.at[step, p], to)
 
     def b_spread_here(step, p):
         _, _, slot = at.b_peer(step)
         return pltpu.make_async_copy(b_slot(slot, p), b_final(step, p), b_got.at[step, p])
 
     def b_twin(step, to, p):
-        return remote(b_final(step, p), b_final(to, p), b_twins.at[to // 2, p], b_got.at[to, p], at.twin)
+        return remote(b_final(step, p), b_final(to, p), b_twins.at[to // 2, whole(p)], b_got.at[to, p], at.twin)
 
     def b_wait(step, p):
         pltpu.make_async_copy(b_final(step, p), b_final(step, p), b_got.at[step, p]).wait()
+
+    def b_wait_whole(step, p):
+        for q in (NB,) if p is NB else range(NP):
+            b_wait(step, q)
 
     barrier = pltpu.get_barrier_semaphore()
 
@@ -224,6 +228,9 @@
         greet_if((source[0] != i) & ((at.core == 1) | (step != 3)), source)
         away = away + jnp.where(at.b_direct(step) & ~here, 1, 0)
 
+    a_own_table[...] = live_table(a_coord, a_count)
+    b_own_table[...] = live_table(b_coord, b_count)
+
     def keep(p):
         @pl.when(at.own1)
         def _():
@@ -251,12 +258,12 @@
     def leave_far(p):
         b_far(p).start()
 
-    def leave_a(p):
-        @pl.when(at.send1)
+    def leave_a(p, low, high):
+        @pl.when(at.send1 & jnp.where(at.g1 < w, low, high))
         def _():
             a_direct(0, p).start()
 
-        @pl.when(at.send2)
+        @pl.when(at.send2 & jnp.where(at.g2 < w, low, high))
         def _():
             a_direct(1, p).start()
 
@@ -382,17 +389,29 @@
         def _():
             pl.semaphore_signal(above, inc=1, device_id=at.z_peer(w - 1), device_id_type=MESH)
 
-    @pl.when(w < 4)
+    rising = (at.zh == 1) & (w <= 4)
+
+    @pl.when(rising)
     def _():
         from_below()
+        each_piece(lambda p: leave_a(p, True, False))
         from_above()
-
-    @pl.when(w >= 4)
-    def _():
-        from_above()
-        from_below()
-
-    each_piece(leave_a)
+        each_piece(lambda p: leave_a(p, False, True))
+
+    @pl.when(~rising)
+    def _():
+        @pl.when(w < 4)
+        def _():
+            from_below()
+            from_above()
+
+        @pl.when(w >= 4)
+        def _():
+            from_above()
+            from_below()
+
+        each_piece(lambda p: leave_a(p, True, True))
+
     a_first = at.zh == 0
 
     @pl.when(a_first)
@@ -448,42 +467,54 @@
     each_piece(share)
 
     def finish(p):
+        def all_of(ref):
+            return ref(p) if p is NB else ref(pl.ds(0, NB))
+
+        def wait(ref, sem):
+            pltpu.make_async_copy(all_of(ref), all_of(ref), sem).wait()
+
+        k = whole(p)
         for step in range(STEPS):
-            pltpu.make_async_copy(a_final(step, p), a_final(step, p), a_got.at[step, p]).wait()
-        b_wait(1, p)
-        b_wait(3, p)
-        b_twin(0, 1, p).wait_send()
+            wait(lambda q: a_final(step, q), a_got.at[step, k])
+        b_wait_whole(1, p)
+        b_wait_whole(3, p)
+
+        def gone(sem):
+            wait(a_own, sem)
+
+        gone(b_twins.at[0, k])
 
         @pl.when(at.core == 1)
         def _():
-            b_twin(2, 3, p).wait_send()
+            gone(b_twins.at[1, k])
 
         for turn in (1, 2, 3):
-            a_spread(turn, p).wait_send()
+            gone(a_fan.at[turn - 1, k])
         for step in (0, 2, 3):
             _, here, _ = at.b_peer(step)
 
             @pl.when(at.b_direct(step) & ~here)
             def _():
-                b_spread(step, p).wait_send()
-
-        for cond, copy in (
-            (at.send1, lambda: a_direct(0, p)),
-            (at.send2, lambda: a_direct(1, p)),
-            (at.relay1, lambda: a_on(0, p)),
-            (at.relay2, lambda: a_on(1, p)),
-            (at.near, lambda: b_near(p)),
-            (at.far_send, lambda: b_far(p)),
-            (at.pass_on, lambda: b_pass(p)),
-            (at.swap_send, lambda: b_swap(p)),
-            (at.swap_get, lambda: b_swap_on(p)),
+                gone(b_fan.at[step, k])
+
+        for cond, sem in (
+            (at.send1, a_send.at[0, k]),
+            (at.send2, a_send.at[1, k]),
+            (at.relay1, a_relay.at[0, k]),
+            (at.relay2, a_relay.at[1, k]),
+            (at.near, b_send.at[0, k]),
+            (at.far_send, b_send.at[1, k]),
+            (at.pass_on, b_send.at[2, k]),
+            (at.swap_send, b_send.at[1, k]),
+            (at.swap_get, b_send.at[2, k]),
         ):
 
             @pl.when(cond)
             def _():
-                copy().wait_send()
-
-    each_piece(finish)
+                gone(sem)
+
+    finish(0)
+    finish(NB)
 
 
 def move(a_blocks, b_blocks, a_coord, a_count, b_coord, b_count):

time: 58.1 us -> 57.6 us (level)
  the two profiles are of different devices: /device:TPU:403 before, /device:TPU:673 now
where the time goes in v4:
time: 57.6 us; the launch traced here: 57.7 us
  Pallas kernels  56.4 us (98%)
  between operations  1.3 us (2%)
    pallas_call x1, Pallas kernels, move(): pl.pallas_call(move_kernel, out_shape=[panel, panel, table, table], in_sp...  52.9 us
    pallas_call x1, Pallas kernels, product(): pl.pallas_call(product_kernel, out_shape=jax.ShapeDtypeStruct((span, span...  3.44 us

profile of v4, /device:TPU:673, one launch (start us, length us, event | category | flops | bytes accessed | tf_op | source)
XLA Modules:
  0.0 57.7 jit_solution(13404704663061646629)
XLA Ops:
  1.3 52.9 %shard_map.73 = (bf16[4,4,128,128]{3,2,1,0:T(8,128)(2,1)}, bf16[4,4,128,128]{3,2,1,0:T(8,128)(2,1)}, s32[4,1,128]{2,1,0:T(1,128)}, s32[4,1,128]{2,1,0:T(1,128)}) custom-call(bf16[4,128,128]{2,1,0:T(8,128)(2,1)} %a_ref.1, bf16[4,128,128]{2,1,0:T(8,128)(2,1)} %b_ref.1, s32[1,4]{1,0:T(1,128)} %a_coord.1, s32[1,1]{1,0:T(1,128)S(6)} %copy.8.a_count, ...), custom_call_target="tpu_custom_call" | custom-call | tf_op jit(solution)/shard_map/pallas_call | solution.py:527
  54.2 3.4 %shard_map.74 = bf16[512,512]{1,0:T(8,128)(2,1)} custom-call(s32[4,1,128]{2,1,0:T(1,128)} %get-tuple-element.9.a_table, s32[4,1,128]{2,1,0:T(1,128)} %get-tuple-element.10.b_table, s32[4,4]{1,0:T(4,128)} %pattern.1, bf16[4,4,128,128]{3,2,1,0:T(8,128)(2,1)} %get-tuple-element.11.a_ref, bf16[4,4,128,128]{3,2,1,0:T(8,128)(2,1)} %get-tuple-element.12.b_ref), custom_call_target="tpu_custom_call" | custom-call | tf_op jit(solution)/shard_map/pallas_call | solution.py:584
